TPU v7x, 512 devices: a whole 4x4x16 slice. The times are simulated.
512 devices in a mesh: leaf: 16 (over x, y), col: 32 (over z, core).
Axes of the slice: x: 4, y: 4, z: 16, core: 2. Of those that a mesh axis runs over, the one named last changes fastest.
Arguments:
- s_blocks: bfloat16 [1024, 8, 128, 128], P(('leaf', 'col')), may hold values from -0.0059814453 to 0.0059814453
- z_blocks: bfloat16 [1024, 8, 128, 128], P(('leaf', 'col')), may hold values from -1.5 to 1.5
- s_requests: int32 [16, 32, 32, 1], P('leaf', 'col'), may hold values from -1 to 15, as said below
- y_pairs: int32 [1024, 8, 8], P(('leaf', 'col')), may hold values from -1 to 31, as said below
- zt_requests: int32 [16, 32, 32, 1], P('leaf', 'col'), may hold values from -1 to 31, as said below
- d_pairs: int32 [1024, 8, 8], P(('leaf', 'col')), may hold values from -1 to 31, as said below
- d_requests: int32 [16, 32, 32, 1], P('leaf', 'col'), may hold values from -1 to 31, as said below
- e_pairs: int32 [1024, 8, 8], P(('leaf', 'col')), may hold values from -1 to 31, as said below
- z_requests: int32 [16, 32, 32, 1], P('leaf', 'col'), may hold values from -1 to 31, as said below
- z_pairs: int32 [1024, 8, 8], P(('leaf', 'col')), may hold values from -1 to 31, as said below
Outputs:
- z_refined: bfloat16 [1024, 8, 128, 128], P(('leaf', 'col'))
Inputs may be any that keep to these rules, and one draw needn't show every extreme that they name: `s_requests`: entry [l, c, p, q] is -1 or a slot of the S holdings of the device (l, p); the entries of one [l, c, p] are distinct. Every reader has some peer with all 1 entries used, and one reader uses all entries. `zt_requests`: entry [l, c, p, q] is -1 or a slot of the Z holdings of the device (l, p); the entries of one [l, c, p] are distinct. Every reader has some peer with all 1 entries used, and one reader uses all entries. `d_requests`: entry [l, c, p, q] is -1 or a slot of the D holdings of the device (l, p); the entries of one [l, c, p] are distinct. Every reader has some peer with all 1 entries used, and one reader uses all entries. `z_requests`: entry [l, c, p, q] is -1 or a slot of the Z holdings of the device (l, p); the entries of one [l, c, p] are distinct. Every reader has some peer with all 1 entries used, and one reader uses all entries. `y_pairs`: each entry is -1 or the position p + q of an entry of s_requests that is not -1, for the reader holding the column; every such entry is named at least once. `d_pairs`: each entry is -1 or the position p + q of an entry of zt_requests that is not -1, for the reader holding the column; every such entry is named at least once. `e_pairs`: each entry is -1 or the position p + q of an entry of d_requests that is not -1, for the reader holding the column; every such entry is named at least once. `z_pairs`: each entry is -1 or the position p + q of an entry of z_requests that is not -1, for the reader holding the column; every such entry is named at least once.
All inputs are finite; a program needn't handle non-finite values.
Results may differ from a plain program's by a relative error of at most 0.0059.
Values may be sent and summed in bfloat16 or wider, within the bound.
No kernel may reach another device: no remote copies, remote signals or barrier semaphores. Data moves between devices by JAX's collectives and lax.ppermute only.
A program may use at most 64 MiB of HBM per device.

v0:
```python
import jax
import jax.numpy as jnp
from jax import lax
from jax.sharding import PartitionSpec as P


def from_partner(value, axis, apart):
    mask = 2**apart
    pairs = [(source, source ^ mask) for source in range(lax.axis_size(axis))]
    return lax.ppermute(value, axis, pairs)


def pick_blocks(holdings, requests):
    lookup = jnp.maximum(requests, 0)
    blocks = jnp.take(holdings, lookup, axis=0)
    return jnp.where((requests >= 0)[:, :, None, None], blocks, jnp.zeros_like(blocks))


def fetch_blocks(holdings, requests):
    fetched = lax.all_to_all(
        pick_blocks(
            holdings, lax.all_to_all(requests, "col", split_axis=0, concat_axis=0, tiled=True)
        ),
        "col",
        split_axis=0,
        concat_axis=0,
        tiled=True,
    )
    return fetched.reshape((-1,) + holdings.shape[1:])


def block_products(fetched, pair_ids, local_blocks, flipped):
    fetch_count = fetched.shape[0]
    padded = jnp.concatenate([fetched, jnp.zeros((1,) + fetched.shape[1:], fetched.dtype)], axis=0)
    lookup = jnp.where(pair_ids < 0, fetch_count, pair_ids)
    chosen = jnp.take(padded, lookup, axis=0)
    einsum_form = "gabji,gbjk->gaik" if flipped else "gabij,gbjk->gaik"
    return jnp.einsum(einsum_form, chosen, local_blocks, preferred_element_type=jnp.float32)


def on_device(
    s_blocks,
    z_blocks,
    s_requests,
    y_pairs,
    zt_requests,
    d_pairs,
    d_requests,
    e_pairs,
    z_requests,
    z_pairs,
):
    columns, slot_count, block_size = (z_blocks.shape[0], z_blocks.shape[1], z_blocks.shape[2])
    flat_shape = (columns * slot_count, block_size, block_size)
    ask_shape = (s_requests.shape[2], s_requests.shape[3])
    s_asks = s_requests.reshape(ask_shape)
    zt_asks = zt_requests.reshape(ask_shape)
    d_asks = d_requests.reshape(ask_shape)
    z_asks = z_requests.reshape(ask_shape)
    s_own = s_blocks.reshape(flat_shape)
    z_own = z_blocks.reshape(flat_shape)
    z_holdings = jnp.concatenate([z_own, from_partner(z_own, "leaf", 0)], axis=0)
    s_fetched = fetch_blocks(s_own, s_asks)
    zt_fetched = fetch_blocks(z_holdings, zt_asks)
    y_blocks = block_products(s_fetched, y_pairs, z_blocks, False).astype(jnp.bfloat16)
    first_slot = (jnp.arange(slot_count) == 0).astype(jnp.float32)
    identity = first_slot[:, None, None] * jnp.eye(block_size, dtype=jnp.float32)
    d_blocks = (identity - block_products(zt_fetched, d_pairs, y_blocks, True)).astype(jnp.bfloat16)
    d_own = d_blocks.reshape(flat_shape)
    d_holdings = jnp.concatenate([d_own, from_partner(d_own, "leaf", 0)], axis=0)
    d_fetched = fetch_blocks(d_holdings, d_asks)
    z_fetched = fetch_blocks(z_holdings, z_asks)
    square = block_products(d_fetched, e_pairs, d_blocks, False)
    e_blocks = (0.5 * d_blocks.astype(jnp.float32) + 0.375 * square).astype(jnp.bfloat16)
    refined = z_blocks.astype(jnp.float32) + block_products(z_fetched, z_pairs, e_blocks, False)
    return refined.astype(jnp.bfloat16)


def solution(mesh):
    in_specs = (
        P(("leaf", "col"), None, None, None),
        P(("leaf", "col"), None, None, None),
        P("leaf", "col", None, None),
        P(("leaf", "col"), None, None),
        P("leaf", "col", None, None),
        P(("leaf", "col"), None, None),
        P("leaf", "col", None, None),
        P(("leaf", "col"), None, None),
        P("leaf", "col", None, None),
        P(("leaf", "col"), None, None),
    )
    out_specs = P(("leaf", "col"), None, None, None)
    return jax.shard_map(
        on_device, mesh=mesh, in_specs=in_specs, out_specs=out_specs, check_vma=False
    )
```

profile of v0, /device:TPU:1, one launch (start us, length us, event | category | flops | bytes accessed | tf_op | source)
XLA Modules:
  0.0 332.6 jit_solution(10021547487266993231)
XLA Ops:
  1.4 16.8 %all-to-all-start.4 = ((s32[32,1,1]{2,1,0:T(1,128)}), s32[32,1,1]{2,1,0:T(1,128)S(1)}, u32[]{:S(2)}, u32[]{:S(2)}) async-start(s32[32,1,1]{2,1,0:T(1,128)} %copy.20), calls=%async_computation.4 | async-start | bytes 32768 | tf_op jit(solution)/shard_map/all_to_all | solution.py:22
  22.2 7.7 %all-to-all-done.4 = s32[32,1,1]{2,1,0:T(1,128)S(1)} async-done(((s32[32,1,1]{2,1,0:T(1,128)}), s32[32,1,1]{2,1,0:T(1,128)S(1)}, u32[]{:S(2)}, u32[]{:S(2)}) %all-to-all-start.4) | async-done | bytes 160 | tf_op jit(solution)/shard_map/all_to_all | solution.py:22
  29.9 4.5 %all-to-all-start.2 = ((s32[32,1,1]{2,1,0:T(1,128)}), s32[32,1,1]{2,1,0:T(1,128)S(1)}, u32[]{:S(2)}, u32[]{:S(2)}) async-start(s32[32,1,1]{2,1,0:T(1,128)} %copy.18), calls=%async_computation.2 | async-start | bytes 32768 | tf_op jit(solution)/shard_map/all_to_all | solution.py:22
  36.3 9.9 %all-to-all-done.2 = s32[32,1,1]{2,1,0:T(1,128)S(1)} async-done(((s32[32,1,1]{2,1,0:T(1,128)}), s32[32,1,1]{2,1,0:T(1,128)S(1)}, u32[]{:S(2)}, u32[]{:S(2)}) %all-to-all-start.2) | async-done | bytes 160 | tf_op jit(solution)/shard_map/all_to_all | solution.py:22
  46.2 4.3 %all-to-all-start.6 = ((s32[32,1,1]{2,1,0:T(1,128)}), s32[32,1,1]{2,1,0:T(1,128)S(1)}, u32[]{:S(2)}, u32[]{:S(2)}) async-start(s32[32,1,1]{2,1,0:T(1,128)} %copy.21), calls=%async_computation.6 | async-start | bytes 32768 | tf_op jit(solution)/shard_map/all_to_all | solution.py:22
  51.3 11.1 %all-to-all-done.6 = s32[32,1,1]{2,1,0:T(1,128)S(1)} async-done(((s32[32,1,1]{2,1,0:T(1,128)}), s32[32,1,1]{2,1,0:T(1,128)S(1)}, u32[]{:S(2)}, u32[]{:S(2)}) %all-to-all-start.6) | async-done | bytes 160 | tf_op jit(solution)/shard_map/all_to_all | solution.py:22
  62.4 4.3 %all-to-all-start = ((s32[32,1,1]{2,1,0:T(1,128)}), s32[32,1,1]{2,1,0:T(1,128)S(1)}, u32[]{:S(2)}, u32[]{:S(2)}) async-start(s32[32,1,1]{2,1,0:T(1,128)} %copy.17), calls=%async_computation | async-start | bytes 32768 | tf_op jit(solution)/shard_map/all_to_all | solution.py:22
  67.9 10.6 %all-to-all-done = s32[32,1,1]{2,1,0:T(1,128)S(1)} async-done(((s32[32,1,1]{2,1,0:T(1,128)}), s32[32,1,1]{2,1,0:T(1,128)S(1)}, u32[]{:S(2)}, u32[]{:S(2)}) %all-to-all-start) | async-done | bytes 160 | tf_op jit(solution)/shard_map/all_to_all | solution.py:22
  78.5 4.5 %all-to-all-start.5 = ((bf16[32,1,128,128]{3,2,1,0:T(8,128)(2,1)}), bf16[32,1,128,128]{3,2,1,0:T(8,128)(2,1)S(1)}, u32[]{:S(2)}, u32[]{:S(2)}) async-start(bf16[32,1,128,128]{3,2,1,0:T(8,128)(2,1)} %fusion.59), calls=%async_computation.5 | async-start | bytes 2097152 | tf_op jit(solution)/shard_map/all_to_all | solution.py:20
  83.0 3.2 collective-permute-start
  87.6 10.5 %collective-permute-done = bf16[16,128,128]{2,1,0:T(8,128)(2,1)S(1)} collective-permute-done((bf16[16,128,128]{2,1,0:T(8,128)(2,1)S(1)}, bf16[16,128,128]{2,1,0:T(8,128)(2,1)S(1)}, u32[]{:S(2)}, u32[]{:S(2)}) %collective-permute-start) | collective-permute-done | bytes 524320 | tf_op jit(solution)/shard_map/ppermute | solution.py:10
  98.2 1.7 gather_fusion.3
  99.9 2.5 fusion.60
  102.3 36.5 %all-to-all-done.5 = bf16[32,1,128,128]{3,2,1,0:T(8,128)(2,1)S(1)} async-done(((bf16[32,1,128,128]{3,2,1,0:T(8,128)(2,1)}), bf16[32,1,128,128]{3,2,1,0:T(8,128)(2,1)S(1)}, u32[]{:S(2)}, u32[]{:S(2)}) %all-to-all-start.5) | async-done | bytes 1048608 | tf_op jit(solution)/shard_map/all_to_all | solution.py:20
  138.8 5.3 %all-to-all-start.3 = ((bf16[32,1,128,128]{3,2,1,0:T(8,128)(2,1)}), bf16[32,1,128,128]{3,2,1,0:T(8,128)(2,1)}, u32[]{:S(2)}, u32[]{:S(2)}) async-start(bf16[32,1,128,128]{3,2,1,0:T(8,128)(2,1)} %fusion.60), calls=%async_computation.3 | async-start | bytes 2097152 | tf_op jit(solution)/shard_map/all_to_all | solution.py:20
  145.5 1.7 gather_fusion.1
  147.2 2.5 fusion.61
  149.6 50.3 %all-to-all-done.3 = bf16[32,1,128,128]{3,2,1,0:T(8,128)(2,1)} async-done(((bf16[32,1,128,128]{3,2,1,0:T(8,128)(2,1)}), bf16[32,1,128,128]{3,2,1,0:T(8,128)(2,1)}, u32[]{:S(2)}, u32[]{:S(2)}) %all-to-all-start.3) | async-done | bytes 1048608 | tf_op jit(solution)/shard_map/all_to_all | solution.py:20
  200.0 4.6 %all-to-all-start.1 = ((bf16[32,1,128,128]{3,2,1,0:T(8,128)(2,1)}), bf16[32,1,128,128]{3,2,1,0:T(8,128)(2,1)S(1)}, u32[]{:S(2)}, u32[]{:S(2)}) async-start(bf16[32,1,128,128]{3,2,1,0:T(8,128)(2,1)} %fusion.61), calls=%async_computation.1 | async-start | bytes 2097152 | tf_op jit(solution)/shard_map/all_to_all | solution.py:20
  207.0 3.0 gather_fusion.5
  211.3 3.0 gather_fusion.4
  214.4 6.3 %copy.19 = bf16[2,8,8,128,128]{3,4,2,1,0:T(8,128)(2,1)} copy(bf16[2,8,8,128,128]{4,3,2,1,0:T(8,128)(2,1)} %bitcast.122) | data formatting | bytes 8388608 | tf_op jit(solution)/shard_map/jit(_take)/gather | solution.py:36
  220.7 5.8 %fusion.49 = bf16[2,8,128,128]{3,2,1,0:T(8,128)(2,1)S(1)} fusion(bf16[2,8,8,128,128]{3,4,2,1,0:T(8,128)(2,1)} %copy.19, pred[2,8,8]{2,1,0:T(8,128)(4,1)S(1)} %get-tuple-element.10, bf16[2,8,8,128,128]{4,3,2,1,0:T(8,128)(2,1)} %bitcast.124, pred[2,8,8]{2,1,0:T(8,128)(4,1)S(1)} %get-tuple-element.9, bf16[2,8,128,128]{3,2,1,0:T(8,128)(2,1)S(1)} %copy-done.3, ...), kind=kOutput, calls=%fused_computation.35 | convolution fusion | flops 1078722560 | bytes 9961728 | tf_op jit(solution)/shard_map/gabji,gbjk->gaik/dot_general | solution.py:38
  226.6 3.2 collective-permute-start.1
  230.5 10.9 %collective-permute-done.1 = bf16[16,128,128]{2,1,0:T(8,128)(2,1)S(1)} collective-permute-done((bf16[16,128,128]{2,1,0:T(8,128)(2,1)S(1)}, bf16[16,128,128]{2,1,0:T(8,128)(2,1)S(1)}, u32[]{:S(2)}, u32[]{:S(2)}) %collective-permute-start.1) | collective-permute-done | bytes 524320 | tf_op jit(solution)/shard_map/ppermute | solution.py:10
  244.2 2.4 fusion.58
  246.7 13.7 %all-to-all-done.1 = bf16[32,1,128,128]{3,2,1,0:T(8,128)(2,1)S(1)} async-done(((bf16[32,1,128,128]{3,2,1,0:T(8,128)(2,1)}), bf16[32,1,128,128]{3,2,1,0:T(8,128)(2,1)S(1)}, u32[]{:S(2)}, u32[]{:S(2)}) %all-to-all-start.1) | async-done | bytes 1048608 | tf_op jit(solution)/shard_map/all_to_all | solution.py:20
  260.4 5.3 %all-to-all-start.7 = ((bf16[32,1,128,128]{3,2,1,0:T(8,128)(2,1)}), bf16[32,1,128,128]{3,2,1,0:T(8,128)(2,1)}, u32[]{:S(2)}, u32[]{:S(2)}) async-start(bf16[32,1,128,128]{3,2,1,0:T(8,128)(2,1)} %fusion.58), calls=%async_computation.7 | async-start | bytes 2097152 | tf_op jit(solution)/shard_map/all_to_all | solution.py:20
  266.1 3.0 gather_fusion.2
  269.1 52.4 %all-to-all-done.7 = bf16[32,1,128,128]{3,2,1,0:T(8,128)(2,1)} async-done(((bf16[32,1,128,128]{3,2,1,0:T(8,128)(2,1)}), bf16[32,1,128,128]{3,2,1,0:T(8,128)(2,1)}, u32[]{:S(2)}, u32[]{:S(2)}) %all-to-all-start.7) | async-done | bytes 1048608 | tf_op jit(solution)/shard_map/all_to_all | solution.py:20
  322.9 3.1 gather_fusion.7
  326.0 6.6 %fusion.46 = bf16[2,8,128,128]{3,2,1,0:T(8,128)(2,1)} fusion(bf16[2,8,8,128,128]{4,3,2,1,0:T(8,128)(2,1)} %bitcast.123, pred[2,8,8]{2,1,0:T(8,128)(4,1)S(1)} %get-tuple-element.12, bf16[2,8,128,128]{3,2,1,0:T(8,128)(2,1)S(1)} %copy-done.4, bf16[2,8,8,128,128]{4,3,2,1,0:T(8,128)(2,1)} %bitcast.125, pred[2,8,8]{2,1,0:T(8,128)(4,1)S(1)} %get-tuple-element.11, ...), kind=kOutput, calls=%fused_computation.34 | convolution fusion | flops 1080033280 | bytes 9961728 | tf_op jit(solution)/shard_map/gabij,gbjk->gaik/dot_general | solution.py:38
  (70 shorter events, 20.9 us)
Async XLA Ops:
  0.0 50.5 %copy-start = (bf16[2,8,128,128]{3,2,1,0:T(8,128)(2,1)S(1)}, bf16[2,8,128,128]{3,2,1,0:T(8,128)(2,1)}, u32[]{:S(2)}) copy-start(bf16[2,8,128,128]{3,2,1,0:T(8,128)(2,1)} %param.14) | copy-start | bytes 1572868
  0.0 83.0 %copy-start.2 = (bf16[2,8,128,128]{3,2,1,0:T(8,128)(2,1)S(1)}, bf16[2,8,128,128]{3,2,1,0:T(8,128)(2,1)}, u32[]{:S(2)}) copy-start(bf16[2,8,128,128]{3,2,1,0:T(8,128)(2,1)} %param.15) | copy-start | bytes 1572868
  1.4 28.5 %all-to-all-start.4 = ((s32[32,1,1]{2,1,0:T(1,128)}), s32[32,1,1]{2,1,0:T(1,128)S(1)}, u32[]{:S(2)}, u32[]{:S(2)}) async-start(s32[32,1,1]{2,1,0:T(1,128)} %copy.20), calls=%async_computation.4 | async-start | bytes 32768 | tf_op jit(solution)/shard_map/all_to_all | solution.py:22
  29.9 16.2 %all-to-all-start.2 = ((s32[32,1,1]{2,1,0:T(1,128)}), s32[32,1,1]{2,1,0:T(1,128)S(1)}, u32[]{:S(2)}, u32[]{:S(2)}) async-start(s32[32,1,1]{2,1,0:T(1,128)} %copy.18), calls=%async_computation.2 | async-start | bytes 32768 | tf_op jit(solution)/shard_map/all_to_all | solution.py:22
  46.2 16.2 %all-to-all-start.6 = ((s32[32,1,1]{2,1,0:T(1,128)}), s32[32,1,1]{2,1,0:T(1,128)S(1)}, u32[]{:S(2)}, u32[]{:S(2)}) async-start(s32[32,1,1]{2,1,0:T(1,128)} %copy.21), calls=%async_computation.6 | async-start | bytes 32768 | tf_op jit(solution)/shard_map/all_to_all | solution.py:22
  62.4 16.1 %all-to-all-start = ((s32[32,1,1]{2,1,0:T(1,128)}), s32[32,1,1]{2,1,0:T(1,128)S(1)}, u32[]{:S(2)}, u32[]{:S(2)}) async-start(s32[32,1,1]{2,1,0:T(1,128)} %copy.17), calls=%async_computation | async-start | bytes 32768 | tf_op jit(solution)/shard_map/all_to_all | solution.py:22
  78.5 60.3 %all-to-all-start.5 = ((bf16[32,1,128,128]{3,2,1,0:T(8,128)(2,1)}), bf16[32,1,128,128]{3,2,1,0:T(8,128)(2,1)S(1)}, u32[]{:S(2)}, u32[]{:S(2)}) async-start(bf16[32,1,128,128]{3,2,1,0:T(8,128)(2,1)} %fusion.59), calls=%async_computation.5 | async-start | bytes 2097152 | tf_op jit(solution)/shard_map/all_to_all | solution.py:20
  83.0 15.1 %collective-permute-start = (bf16[16,128,128]{2,1,0:T(8,128)(2,1)S(1)}, bf16[16,128,128]{2,1,0:T(8,128)(2,1)S(1)}, u32[]{:S(2)}, u32[]{:S(2)}) collective-permute-start(bf16[16,128,128]{2,1,0:T(8,128)(2,1)S(1)} %bitcast.128), channel_id=1, source_target_pairs={{0,32},{32,0},{64,96},{96,64},{128,160},{160,128},{192,224},{224,1... | collective-permute-start | bytes 1572872 | tf_op jit(solution)/shard_map/ppermute | solution.py:10
  102.3 102.3 %copy-start.7 = (s32[2,8,8]{2,1,0:T(8,128)S(1)}, s32[2,8,8]{2,1,0:T(8,128)}, u32[]{:S(2)}) copy-start(s32[2,8,8]{2,1,0:T(8,128)} %param.19) | copy-start | bytes 1540
  102.3 102.4 %copy-start.8 = (s32[2,8,8]{2,1,0:T(8,128)S(1)}, s32[2,8,8]{2,1,0:T(8,128)}, u32[]{:S(2)}) copy-start(s32[2,8,8]{2,1,0:T(8,128)} %param.17) | copy-start | bytes 1540
  138.8 61.2 %copy-start.1 = (bf16[32,1,128,128]{3,2,1,0:T(8,128)(2,1)}, bf16[32,1,128,128]{3,2,1,0:T(8,128)(2,1)S(1)}, u32[]{:S(2)}) copy-start(bf16[32,1,128,128]{3,2,1,0:T(8,128)(2,1)S(1)} %all-to-all-done.5) | copy-start | bytes 3145732
  138.8 61.1 %all-to-all-start.3 = ((bf16[32,1,128,128]{3,2,1,0:T(8,128)(2,1)}), bf16[32,1,128,128]{3,2,1,0:T(8,128)(2,1)}, u32[]{:S(2)}, u32[]{:S(2)}) async-start(bf16[32,1,128,128]{3,2,1,0:T(8,128)(2,1)} %fusion.60), calls=%async_computation.3 | async-start | bytes 2097152 | tf_op jit(solution)/shard_map/all_to_all | solution.py:20
  200.0 60.4 %all-to-all-start.1 = ((bf16[32,1,128,128]{3,2,1,0:T(8,128)(2,1)}), bf16[32,1,128,128]{3,2,1,0:T(8,128)(2,1)S(1)}, u32[]{:S(2)}, u32[]{:S(2)}) async-start(bf16[32,1,128,128]{3,2,1,0:T(8,128)(2,1)} %fusion.61), calls=%async_computation.1 | async-start | bytes 2097152 | tf_op jit(solution)/shard_map/all_to_all | solution.py:20
  214.4 6.3 %copy-start.3 = (bf16[2,8,128,128]{3,2,1,0:T(8,128)(2,1)S(1)}, bf16[2,8,128,128]{3,2,1,0:T(8,128)(2,1)}, u32[]{:S(2)}) copy-start(bf16[2,8,128,128]{3,2,1,0:T(8,128)(2,1)} %param.15) | copy-start | bytes 1572868
  226.5 3.9 %copy-start.5 = (bf16[2,8,128,128]{3,2,1,0:T(8,128)(2,1)}, bf16[2,8,128,128]{3,2,1,0:T(8,128)(2,1)S(1)}, u32[]{:S(2)}) copy-start(bf16[2,8,128,128]{3,2,1,0:T(8,128)(2,1)S(1)} %fusion.49) | copy-start | bytes 1572868
  226.6 14.9 %collective-permute-start.1 = (bf16[16,128,128]{2,1,0:T(8,128)(2,1)S(1)}, bf16[16,128,128]{2,1,0:T(8,128)(2,1)S(1)}, u32[]{:S(2)}, u32[]{:S(2)}) collective-permute-start(bf16[16,128,128]{2,1,0:T(8,128)(2,1)S(1)} %bitcast.130), channel_id=1, source_target_pairs={{0,32},{32,0},{64,96},{96,64},{128,160},{160,128},{192,224},{224,1... | collective-permute-start | bytes 1572872 | tf_op jit(solution)/shard_map/ppermute | solution.py:10
  230.5 35.2 %copy-start.10 = (s32[2,8,8]{2,1,0:T(8,128)S(1)}, s32[2,8,8]{2,1,0:T(8,128)}, u32[]{:S(2)}) copy-start(s32[2,8,8]{2,1,0:T(8,128)} %param.21) | copy-start | bytes 1540
  230.5 35.3 %copy-start.9 = (s32[2,8,8]{2,1,0:T(8,128)S(1)}, s32[2,8,8]{2,1,0:T(8,128)}, u32[]{:S(2)}) copy-start(s32[2,8,8]{2,1,0:T(8,128)} %param.23) | copy-start | bytes 1540
  260.4 61.2 %all-to-all-start.7 = ((bf16[32,1,128,128]{3,2,1,0:T(8,128)(2,1)}), bf16[32,1,128,128]{3,2,1,0:T(8,128)(2,1)}, u32[]{:S(2)}, u32[]{:S(2)}) async-start(bf16[32,1,128,128]{3,2,1,0:T(8,128)(2,1)} %fusion.58), calls=%async_computation.7 | async-start | bytes 2097152 | tf_op jit(solution)/shard_map/all_to_all | solution.py:20
  322.9 3.1 copy-start.4
  322.9 3.1 copy-start.6
where the time goes:
time: 334 us; the launch traced here: 333 us
  waiting for transfers between devices  214 us (64%)
  starting transfers between devices  55.9 us (17%)
  local copies, waits for them, and re-layouts  34.2 us (10%)
  other arithmetic  15.9 us (5%)
  matrix products  12.5 us (4%)
    all_to_all x4, waiting for transfers between devices, fetch_blocks(): lax.all_to_all(pick_blocks(holdings, lax.all_to_all(requests, 'col', spli...  153 us
    all_to_all x4, waiting for transfers between devices, fetch_blocks(): lax.all_to_all(requests, 'col', split_axis=0, concat_axis=0, tiled=True)  39.4 us
    all_to_all x4, starting transfers between devices, fetch_blocks(): lax.all_to_all(requests, 'col', split_axis=0, concat_axis=0, tiled=True)  29.9 us
    ppermute x2, waiting for transfers between devices, from_partner(): return lax.ppermute(value, axis, pairs)  21.4 us
    all_to_all x4, starting transfers between devices, fetch_blocks(): lax.all_to_all(pick_blocks(holdings, lax.all_to_all(requests, 'col', spli...  19.6 us
    gather x5, local copies, waits for them, and re-layouts, block_products(): chosen = jnp.take(padded, lookup, axis=0)  18.4 us
    dot_general x2, matrix products, block_products(): jnp.einsum(einsum_form, chosen, local_blocks, preferred_element_type=jnp....  12.5 us
    select_n x4, other arithmetic, pick_blocks(): jnp.where((requests >= 0)[:, :, None, None], blocks, jnp.zeros_like(blocks))  8.52 us
  transfers between devices with their start and end apart: 10, of which 10 were waited for; matrix products, arithmetic and copies ran while one was open for 15% of the time, Pallas kernels for 0%

commit v1 on v0

v1 whole, which is shorter than its diff:
```python
import functools

import jax
import jax.numpy as jnp
from jax import lax
from jax.experimental import pallas as pl
from jax.experimental.pallas import tpu as pltpu
from jax.sharding import PartitionSpec as P

BF16 = jnp.bfloat16
F32 = jnp.float32
SMEM = pl.BlockSpec(memory_space=pltpu.SMEM)
VMEM = pl.BlockSpec(memory_space=pltpu.VMEM)
ANY = pl.BlockSpec(memory_space=pl.ANY)


def from_partner(value):
    pairs = [(source, source ^ 1) for source in range(lax.axis_size("leaf"))]
    return lax.ppermute(value, "leaf", pairs)


def exchange(value):
    return lax.all_to_all(value, "col", split_axis=0, concat_axis=0, tiled=True)


def pick_kernel(lists, asks, *refs):
    sources = 1 + max(h for _, held in lists for h in held)
    held_refs, out, zero, sem = refs[:sources], refs[sources], refs[-2], refs[-1]
    zero[...] = jnp.zeros_like(zero)
    readers = out.shape[0]

    @pl.loop(0, readers)
    def _(reader):
        for place, (row, held) in enumerate(lists):
            slot = asks[reader, row]
            target = out.at[reader, place]

            @pl.when(slot < 0)
            def _():
                pltpu.make_async_copy(zero, target, sem).start()

            first = 0
            for h in held:
                count = held_refs[h].shape[0]

                @pl.when((slot >= first) & (slot < first + count))
                def _():
                    pltpu.make_async_copy(held_refs[h].at[slot - first], target, sem).start()

                first += count

    pltpu.make_async_copy(out, out, sem).wait()


def pick(asks, holdings, lists, name):
    block = holdings[0].shape[1:]
    shape = (asks.shape[0], len(lists)) + block
    size = 2 * shape[0] * shape[1] * shape[2] * shape[3]
    return pl.pallas_call(
        functools.partial(pick_kernel, lists),
        out_shape=jax.ShapeDtypeStruct(shape, BF16),
        in_specs=[SMEM] + [VMEM] * len(holdings),
        out_specs=ANY,
        scratch_shapes=[pltpu.VMEM(block, BF16), pltpu.SemaphoreType.DMA],
        cost_estimate=pl.CostEstimate(flops=0, bytes_accessed=4 * size, transcendentals=0),
        name=name,
    )(asks, *holdings)


def gather_rows(pairs, blocks, g, wide):
    slots, count = pairs.shape[1], blocks.shape[0] - 1
    size = blocks.shape[1]

    @pl.loop(0, slots)
    def _(a):
        for b in range(slots):
            pair = pairs[g, a, b]
            at = jnp.where(pair < 0, count, pair)
            row = pl.multiple_of(a * size, size)
            wide[pl.ds(row, size), b * size : (b + 1) * size] = blocks[at]


def product(pairs, blocks, g, wide, right):
    gather_rows(pairs, blocks, g, wide)
    tall = right.reshape(right.shape[0] * right.shape[1], right.shape[2])
    return jnp.dot(wide[...], tall, preferred_element_type=F32)


def yd_kernel(y_pairs, d_pairs, fetched, z, d, s_in, zt_in, wide, y, sems):
    count = fetched.shape[0]
    slots, size = z.shape[1], z.shape[2]
    copies = [
        pltpu.make_async_copy(fetched.at[:, i], into.at[pl.ds(0, count)], sems.at[i])
        for i, into in enumerate((s_in, zt_in))
    ]
    for copy in copies:
        copy.start()
    s_in[count] = jnp.zeros((size, size), BF16)
    zt_in[count] = jnp.zeros((size, size), BF16)
    copies[0].wait()
    for g in range(z.shape[0]):
        y[g] = product(y_pairs, s_in, g, wide, z[g]).astype(BF16).reshape(slots, size, size)
    copies[1].wait()

    @pl.loop(0, count)
    def _(i):
        zt_in[i] = zt_in[i].T

    rows = lax.broadcasted_iota(jnp.int32, (slots * size, size), 0)
    columns = lax.broadcasted_iota(jnp.int32, (slots * size, size), 1)
    for g in range(z.shape[0]):
        total = product(d_pairs, zt_in, g, wide, y[g])
        total = jnp.where(rows == columns, 1.0, 0.0) - total
        d[g] = total.astype(BF16).reshape(slots, size, size)


def ez_kernel(e_pairs, z_pairs, d_fetched, z_fetched, d, z, out, d_in, z_in, wide, e, sems):
    count = d_fetched.shape[0]
    slots, size = z.shape[1], z.shape[2]
    copies = [
        pltpu.make_async_copy(src.at[:, 0], into.at[pl.ds(0, count)], sems.at[i])
        for i, (src, into) in enumerate(((d_fetched, d_in), (z_fetched, z_in)))
    ]
    for copy in copies:
        copy.start()
    d_in[count] = jnp.zeros((size, size), BF16)
    z_in[count] = jnp.zeros((size, size), BF16)
    copies[0].wait()
    tall = (slots * size, size)
    for g in range(z.shape[0]):
        square = product(e_pairs, d_in, g, wide, d[g])
        mixed = 0.5 * d[g].reshape(tall).astype(F32) + 0.375 * square
        e[g] = mixed.astype(BF16).reshape(slots, size, size)
    copies[1].wait()
    for g in range(z.shape[0]):
        total = z[g].reshape(tall).astype(F32) + product(z_pairs, z_in, g, wide, e[g])
        out[g] = total.astype(BF16).reshape(slots, size, size)


def paired_call(body, name, pairs, fetched, local):
    columns, slots, size = local[0].shape[:3]
    count = fetched[0].shape[0]
    flops = 4 * columns * slots * slots * size**3
    return pl.pallas_call(
        body,
        out_shape=jax.ShapeDtypeStruct(local[0].shape, BF16),
        in_specs=[SMEM] * 2 + [ANY] * len(fetched) + [VMEM] * len(local),
        out_specs=VMEM,
        scratch_shapes=[
            pltpu.VMEM((count + 1, size, size), BF16),
            pltpu.VMEM((count + 1, size, size), BF16),
            pltpu.VMEM((slots * size, slots * size), BF16),
            pltpu.VMEM(local[0].shape, BF16),
            pltpu.SemaphoreType.DMA((2,)),
        ],
        compiler_params=pltpu.CompilerParams(vmem_limit_bytes=32 * 2**20),
        cost_estimate=pl.CostEstimate(flops=flops, bytes_accessed=16 * 2**20, transcendentals=0),
        name=name,
    )(*pairs, *fetched, *local)


def on_device(
    s_blocks, z_blocks, s_requests, y_pairs, zt_requests, d_pairs, d_requests, e_pairs, z_requests, z_pairs
):
    flat_shape = (-1,) + z_blocks.shape[2:]
    peers = s_requests.shape[2]
    wanted = [r.reshape(peers, 1) for r in (s_requests, zt_requests, z_requests, d_requests)]
    asks = exchange(jnp.concatenate(wanted, axis=1))
    s_own = s_blocks.reshape(flat_shape)
    z_own = z_blocks.reshape(flat_shape)
    z_other = from_partner(z_own)
    first = pick(asks, (s_own, z_own, z_other), ((0, (0,)), (1, (1, 2))), "pick_s_zt")
    second = pick(asks, (z_own, z_other), ((2, (0, 1)),), "pick_z")
    first = exchange(first)
    first, second = lax.optimization_barrier((first, second))
    z_fetched = exchange(second)
    d_blocks = paired_call(yd_kernel, "make_d", (y_pairs, d_pairs), (first,), (z_blocks,))
    d_own = d_blocks.reshape(flat_shape)
    d_other = from_partner(d_own)
    third = pick(asks, (d_own, d_other), ((3, (0, 1)),), "pick_d")
    d_fetched = exchange(third)
    return paired_call(ez_kernel, "refine", (e_pairs, z_pairs), (d_fetched, z_fetched), (d_blocks, z_blocks))


def solution(mesh):
    blocks = P(("leaf", "col"), None, None, None)
    requests = P("leaf", "col", None, None)
    pairs = P(("leaf", "col"), None, None)
    in_specs = (blocks, blocks) + (requests, pairs) * 4
    return jax.shard_map(on_device, mesh=mesh, in_specs=in_specs, out_specs=blocks, check_vma=False)
```

time: 334 us -> 271 us (0.81)
  blocking collectives: 0 us -> 88.3 us
  waiting for transfers between devices: 214 us -> 137 us
  starting transfers between devices: 55.9 us -> 17.4 us
  local copies, waits for them, and re-layouts: 34.2 us -> 1.73 us
  Pallas kernels: 0 us -> 25.4 us
  other arithmetic: 15.9 us -> 0.72 us
  matrix products: 12.5 us -> 0 us
    all_to_all x0 -> x2, blocking collectives: none -> 88.3 us  [exchange(): return lax.all_to_all(value, 'col', split_axis=0, concat_axis=0, tiled=True)]
    all_to_all x8 -> x2, waiting for transfers between devices: 192 us -> 124 us  [exchange(): return lax.all_to_all(value, 'col', split_axis=0, concat_axis=0, tiled=True)]
    all_to_all x8 -> x2, starting transfers between devices: 49.5 us -> 11.2 us  [exchange(): return lax.all_to_all(value, 'col', split_axis=0, concat_axis=0, tiled=True)]
    pallas_call x0 -> x5, Pallas kernels: none -> 25.4 us  [the longest x2 18.2 us: paired_call(): pl.pallas_call(body, out_shape=jax.ShapeDtypeStruct(local[0].shape, BF16)...]
    gather x9 -> x0, local copies, waits for them, and re-layouts: 24.3 us -> none  [the longest x5 18.4 us: block_products(): chosen = jnp.take(padded, lookup, axis=0)]
    dot_general x2 -> x0, matrix products: 12.5 us -> none  [block_products(): jnp.einsum(einsum_form, chosen, local_blocks, preferred_element_type=jnp....]
    select_n x8 -> x0, other arithmetic: 8.54 us -> none  [the longest x4 8.52 us: pick_blocks(): jnp.where((requests >= 0)[:, :, None, None], blocks, jnp.zeros_like(blocks))]
    ppermute x2, waiting for transfers between devices: 21.4 us -> 12.9 us  [from_partner(): return lax.ppermute(value, 'leaf', pairs)]
  transfers between devices with their start and end apart: 10 -> 4, of which waited for: 10 -> 3; matrix products, arithmetic and copies ran while one was open for 15% -> 0% of each run, Pallas kernels for 0% -> 5%
where the time goes in v1:
time: 271 us
  waiting for transfers between devices  137 us (51%)
  blocking collectives  88.3 us (33%)
  Pallas kernels  25.4 us (9%)
  starting transfers between devices  17.4 us (6%)
    all_to_all x2, waiting for transfers between devices, exchange(): return lax.all_to_all(value, 'col', split_axis=0, concat_axis=0, tiled=True)  124 us
    all_to_all x2, blocking collectives, exchange(): return lax.all_to_all(value, 'col', split_axis=0, concat_axis=0, tiled=True)  88.3 us
    pallas_call x2, Pallas kernels, paired_call(): pl.pallas_call(body, out_shape=jax.ShapeDtypeStruct(local[0].shape, BF16)...  18.2 us
    ppermute x2, waiting for transfers between devices, from_partner(): return lax.ppermute(value, 'leaf', pairs)  12.9 us
    all_to_all x2, starting transfers between devices, exchange(): return lax.all_to_all(value, 'col', split_axis=0, concat_axis=0, tiled=True)  11.2 us
    pallas_call x3, Pallas kernels, pick(): pl.pallas_call(functools.partial(pick_kernel, lists), out_shape=jax.Shape...  7.25 us
    ppermute x2, starting transfers between devices, from_partner(): return lax.ppermute(value, 'leaf', pairs)  6.23 us
  transfers between devices with their start and end apart: 4, of which 3 were waited for; matrix products, arithmetic and copies ran while one was open for 0% of the time, Pallas kernels for 5%

profile of v1, /device:TPU:1, one launch (start us, length us, event | category | flops | bytes accessed | tf_op | source)
XLA Modules:
  0.0 270.9 jit_solution(1397725255089796095)
XLA Ops:
  0.0 4.0 %collective-permute-start = (bf16[16,128,128]{2,1,0:T(8,128)(2,1)}, bf16[16,128,128]{2,1,0:T(8,128)(2,1)S(1)}, u32[]{:S(2)}, u32[]{:S(2)}) collective-permute-start(bf16[16,128,128]{2,1,0:T(8,128)(2,1)} %bitcast.10), channel_id=1, source_target_pairs={{0,32},{32,0},{64,96},{96,64},{128,160},{160,128},{192,224},{224,1... | collective-permute-start | bytes 1572872 | tf_op jit(solution)/shard_map/ppermute | solution.py:19
  4.0 0.7 add_bitcast_fusion
  4.7 0.1 copy.14
  4.8 27.9 %all_to_all.26 = s32[32,1,4]{2,1,0:T(1,128)} all-to-all(s32[32,1,4]{2,1,0:T(1,128)S(1)} %copy.14), channel_id=1, replica_groups=mesh['leaf'=16,'col'=32] {'col'}, dimensions={0} | all-to-all | bytes 1024 | tf_op jit(solution)/shard_map/all_to_all | solution.py:23
  32.7 0.0 collective-permute-done.refs_2_.refs_1_
  32.7 0.8 copy-done.7
  33.5 2.7 %pick_s_zt.1 = bf16[32,2,128,128]{3,2,1,0:T(8,128)(2,1)} custom-call(s32[32,4]{1,0:T(8,128)} %bitcast.16, bf16[16,128,128]{2,1,0:T(8,128)(2,1)} %bitcast.15, bf16[16,128,128]{2,1,0:T(8,128)(2,1)} %bitcast.11, bf16[16,128,128]{2,1,0:T(8,128)(2,1)} %copy-done.7), custom_call_target="tpu_custom_call" | custom-call | bytes 8388608 | tf_op jit(solution)/shard_map/pick_s_zt/pallas_call | solution.py:59
  36.3 4.4 %all-to-all-start.1 = ((bf16[32,2,128,128]{3,2,1,0:T(8,128)(2,1)}), bf16[32,2,128,128]{3,2,1,0:T(8,128)(2,1)S(1)}, u32[]{:S(2)}, u32[]{:S(2)}) async-start(bf16[32,2,128,128]{3,2,1,0:T(8,128)(2,1)} %pick_s_zt.1), calls=%async_computation.1 | async-start | bytes 4194304 | tf_op jit(solution)/shard_map/all_to_all | solution.py:23
  40.7 0.0 copy-start
  40.7 0.0 copy-start.3
  40.7 0.0 copy-start.4
  40.7 2.3 pick_z.1
  43.0 97.0 %all-to-all-done.1.fetched = bf16[32,2,128,128]{3,2,1,0:T(8,128)(2,1)S(1)} async-done(((bf16[32,2,128,128]{3,2,1,0:T(8,128)(2,1)}), bf16[32,2,128,128]{3,2,1,0:T(8,128)(2,1)S(1)}, u32[]{:S(2)}, u32[]{:S(2)}) %all-to-all-start.1) | async-done | bytes 2097184 | tf_op jit(solution)/shard_map/all_to_all | solution.py:23
  140.0 6.7 %all-to-all-start.3 = ((bf16[32,1,128,128]{3,2,1,0:T(8,128)(2,1)}), bf16[32,1,128,128]{3,2,1,0:T(8,128)(2,1)}, u32[]{:S(2)}, u32[]{:S(2)}) async-start(bf16[32,1,128,128]{3,2,1,0:T(8,128)(2,1)} %pick_z.1), calls=%async_computation.3 | async-start | bytes 2097152 | tf_op jit(solution)/shard_map/all_to_all | solution.py:23
  146.7 0.0 copy-done
  146.8 0.0 copy-done.3
  146.8 0.0 copy-done.4
  146.8 10.4 %make_d.1.d = bf16[2,8,128,128]{3,2,1,0:T(8,128)(2,1)S(1)} custom-call(s32[2,8,8]{2,1,0:T(8,128)S(1)} %copy-done.3, s32[2,8,8]{2,1,0:T(8,128)S(1)} %copy-done.4, bf16[32,2,128,128]{3,2,1,0:T(8,128)(2,1)S(1)} %all-to-all-done.1.fetched, bf16[2,8,128,128]{3,2,1,0:T(8,128)(2,1)S(1)} %copy-done), custom_call_target="tpu_custom_call" | custom-call | flops 1073741824 | bytes 16777216 | tf_op jit(solution)/shard_map/make_d/pallas_call | solution.py:144
  157.1 0.0 copy-start.1
  157.1 0.0 copy-start.5
  157.2 0.0 copy-start.6
  157.2 2.2 collective-permute-start.1
  159.4 12.9 %collective-permute-done.1.refs_1_ = bf16[16,128,128]{2,1,0:T(8,128)(2,1)S(1)} collective-permute-done((bf16[16,128,128]{2,1,0:T(8,128)(2,1)S(1)}, bf16[16,128,128]{2,1,0:T(8,128)(2,1)S(1)}, u32[]{:S(2)}, u32[]{:S(2)}) %collective-permute-start.1) | collective-permute-done | bytes 524320 | tf_op jit(solution)/shard_map/ppermute | solution.py:19
  172.3 0.0 copy-done.1
  172.3 0.8 copy-done.8
  173.1 2.2 pick_d.1
  175.3 0.0 copy-start.2
  175.3 27.3 %all-to-all-done.3.z_fetched = bf16[32,1,128,128]{3,2,1,0:T(8,128)(2,1)} async-done(((bf16[32,1,128,128]{3,2,1,0:T(8,128)(2,1)}), bf16[32,1,128,128]{3,2,1,0:T(8,128)(2,1)}, u32[]{:S(2)}, u32[]{:S(2)}) %all-to-all-start.3) | async-done | bytes 1048608 | tf_op jit(solution)/shard_map/all_to_all | solution.py:23
  202.6 60.4 %all_to_all.27.d_fetched = bf16[32,1,128,128]{3,2,1,0:T(8,128)(2,1)S(1)} all-to-all(bf16[32,1,128,128]{3,2,1,0:T(8,128)(2,1)} %pick_d.1), channel_id=1, replica_groups=mesh['leaf'=16,'col'=32] {'col'}, dimensions={0} | all-to-all | bytes 2097152 | tf_op jit(solution)/shard_map/all_to_all | solution.py:23
  263.0 0.0 copy-done.5
  263.0 0.0 copy-done.6
  263.0 7.8 %refine.1 = bf16[2,8,128,128]{3,2,1,0:T(8,128)(2,1)} custom-call(s32[2,8,8]{2,1,0:T(8,128)S(1)} %copy-done.5, s32[2,8,8]{2,1,0:T(8,128)S(1)} %copy-done.6, bf16[32,1,128,128]{3,2,1,0:T(8,128)(2,1)S(1)} %all_to_all.27.d_fetched, bf16[32,1,128,128]{3,2,1,0:T(8,128)(2,1)} %all-to-all-done.3.z_fetched, bf16[2,8,128,128]{3,2,1,0:T(8,128)(2,1)S(1)} %copy-done.2, ...), custom_call_target="tpu_custom_call" | custom-call | flops 1073741824 | bytes 16777216 | tf_op jit(solution)/shard_map/refine/pallas_call | solution.py:144
  (3 shorter events, 0.0 us)
Async XLA Ops:
  0.0 32.7 %collective-permute-start = (bf16[16,128,128]{2,1,0:T(8,128)(2,1)}, bf16[16,128,128]{2,1,0:T(8,128)(2,1)S(1)}, u32[]{:S(2)}, u32[]{:S(2)}) collective-permute-start(bf16[16,128,128]{2,1,0:T(8,128)(2,1)} %bitcast.10), channel_id=1, source_target_pairs={{0,32},{32,0},{64,96},{96,64},{128,160},{160,128},{192,224},{224,1... | collective-permute-start | bytes 1572872 | tf_op jit(solution)/shard_map/ppermute | solution.py:19
  32.7 0.8 copy-start.7
  36.3 103.7 %all-to-all-start.1 = ((bf16[32,2,128,128]{3,2,1,0:T(8,128)(2,1)}), bf16[32,2,128,128]{3,2,1,0:T(8,128)(2,1)S(1)}, u32[]{:S(2)}, u32[]{:S(2)}) async-start(bf16[32,2,128,128]{3,2,1,0:T(8,128)(2,1)} %pick_s_zt.1), calls=%async_computation.1 | async-start | bytes 4194304 | tf_op jit(solution)/shard_map/all_to_all | solution.py:23
  40.7 106.1 %copy-start = (bf16[2,8,128,128]{3,2,1,0:T(8,128)(2,1)S(1)}, bf16[2,8,128,128]{3,2,1,0:T(8,128)(2,1)}, u32[]{:S(2)}) copy-start(bf16[2,8,128,128]{3,2,1,0:T(8,128)(2,1)} %z.3) | copy-start | bytes 1572868
  40.7 106.1 %copy-start.3 = (s32[2,8,8]{2,1,0:T(8,128)S(1)}, s32[2,8,8]{2,1,0:T(8,128)}, u32[]{:S(2)}) copy-start(s32[2,8,8]{2,1,0:T(8,128)} %y_pairs.1) | copy-start | bytes 1540
  40.7 106.0 %copy-start.4 = (s32[2,8,8]{2,1,0:T(8,128)S(1)}, s32[2,8,8]{2,1,0:T(8,128)}, u32[]{:S(2)}) copy-start(s32[2,8,8]{2,1,0:T(8,128)} %d_pairs.1) | copy-start | bytes 1540
  140.0 62.6 %all-to-all-start.3 = ((bf16[32,1,128,128]{3,2,1,0:T(8,128)(2,1)}), bf16[32,1,128,128]{3,2,1,0:T(8,128)(2,1)}, u32[]{:S(2)}, u32[]{:S(2)}) async-start(bf16[32,1,128,128]{3,2,1,0:T(8,128)(2,1)} %pick_z.1), calls=%async_computation.3 | async-start | bytes 2097152 | tf_op jit(solution)/shard_map/all_to_all | solution.py:23
  157.1 15.1 %copy-start.1 = (bf16[2,8,128,128]{3,2,1,0:T(8,128)(2,1)}, bf16[2,8,128,128]{3,2,1,0:T(8,128)(2,1)S(1)}, u32[]{:S(2)}) copy-start(bf16[2,8,128,128]{3,2,1,0:T(8,128)(2,1)S(1)} %make_d.1.d) | copy-start | bytes 1572868
  157.1 105.9 %copy-start.5 = (s32[2,8,8]{2,1,0:T(8,128)S(1)}, s32[2,8,8]{2,1,0:T(8,128)}, u32[]{:S(2)}) copy-start(s32[2,8,8]{2,1,0:T(8,128)} %e_pairs.1) | copy-start | bytes 1540
  157.2 105.9 %copy-start.6 = (s32[2,8,8]{2,1,0:T(8,128)S(1)}, s32[2,8,8]{2,1,0:T(8,128)}, u32[]{:S(2)}) copy-start(s32[2,8,8]{2,1,0:T(8,128)} %z_pairs.1) | copy-start | bytes 1540
  157.2 15.1 %collective-permute-start.1 = (bf16[16,128,128]{2,1,0:T(8,128)(2,1)S(1)}, bf16[16,128,128]{2,1,0:T(8,128)(2,1)S(1)}, u32[]{:S(2)}, u32[]{:S(2)}) collective-permute-start(bf16[16,128,128]{2,1,0:T(8,128)(2,1)S(1)} %bitcast.13), channel_id=1, source_target_pairs={{0,32},{32,0},{64,96},{96,64},{128,160},{160,128},{192,224},{224,1... | collective-permute-start | bytes 1572872 | tf_op jit(solution)/shard_map/ppermute | solution.py:19
  172.3 0.8 copy-start.8
  175.3 87.7 %copy-start.2 = (bf16[2,8,128,128]{3,2,1,0:T(8,128)(2,1)S(1)}, bf16[2,8,128,128]{3,2,1,0:T(8,128)(2,1)}, u32[]{:S(2)}) copy-start(bf16[2,8,128,128]{3,2,1,0:T(8,128)(2,1)} %copy-done.1) | copy-start | bytes 1572868

commit v2 on v1

v2 whole, which is shorter than its diff:
```python
import functools

import jax
import jax.numpy as jnp
from jax import lax
from jax.experimental import pallas as pl
from jax.experimental.pallas import tpu as pltpu
from jax.sharding import PartitionSpec as P

BF16 = jnp.bfloat16
F32 = jnp.float32
SMEM = pl.BlockSpec(memory_space=pltpu.SMEM)
VMEM = pl.BlockSpec(memory_space=pltpu.VMEM)
ANY = pl.BlockSpec(memory_space=pl.ANY)


def from_partner(value):
    pairs = [(source, source ^ 1) for source in range(lax.axis_size("leaf"))]
    return lax.ppermute(value, "leaf", pairs)


def exchange(value):
    return lax.all_to_all(value, "col", split_axis=0, concat_axis=0, tiled=True)


def pick_kernel(lists, asks, *refs):
    sources = max(end for _, _, end in lists)
    held, out = refs[:sources], refs[sources]
    stores, asked, sem, in_sems = refs[sources + 1 : -3], refs[-3], refs[-2], refs[-1]
    readers = out.shape[0]
    ask_copy = pltpu.make_async_copy(asks, asked, in_sems.at[in_sems.shape[0] - 1])
    ask_copy.start()
    copies, sizes = [], []
    for store, (_, begin, end) in zip(stores, lists):
        first = 0
        for h in range(begin, end):
            count = held[h].shape[0]
            copies.append(pltpu.make_async_copy(held[h], store.at[pl.ds(first, count)], in_sems.at[len(copies)]))
            first += count
        sizes.append(first)
    for copy in copies:
        copy.start()
    for store, size in zip(stores, sizes):
        store[size] = jnp.zeros(store.shape[1:], BF16)
    ask_copy.wait()
    for copy in copies:
        copy.wait()

    @pl.loop(0, readers)
    def _(reader):
        for place, (store, size, (row, _, _)) in enumerate(zip(stores, sizes, lists)):
            slot = asked[reader, row]
            at = jnp.where(slot < 0, size, slot)
            pltpu.make_async_copy(store.at[at], out.at[reader, place], sem).start()

    pltpu.make_async_copy(out, out, sem).wait()


def pick(asks, holdings, lists, name):
    block = holdings[0].shape[1:]
    shape = (asks.shape[0], len(lists)) + block
    size = 2 * shape[0] * shape[1] * shape[2] * shape[3]
    stores = [
        pltpu.VMEM((1 + sum(h.shape[0] for h in holdings[begin:end]),) + block, BF16) for _, begin, end in lists
    ]
    return pl.pallas_call(
        functools.partial(pick_kernel, lists),
        out_shape=jax.ShapeDtypeStruct(shape, BF16),
        in_specs=[ANY] * (1 + len(holdings)),
        out_specs=ANY,
        scratch_shapes=[
            *stores,
            pltpu.SMEM(asks.shape, jnp.int32),
            pltpu.SemaphoreType.DMA,
            pltpu.SemaphoreType.DMA((1 + sum(end - begin for _, begin, end in lists),)),
        ],
        cost_estimate=pl.CostEstimate(flops=0, bytes_accessed=3 * size, transcendentals=0),
        name=name,
    )(asks, *holdings)


def product(pairs, blocks, g, a, right):
    slots, last = pairs.shape[2], blocks.shape[0] - 1
    chosen = []
    for b in range(slots):
        pair = pairs[g, a, b]
        chosen.append(blocks[jnp.where(pair < 0, last, pair)])
    tall = right.reshape(right.shape[0] * right.shape[1], right.shape[2])
    return jnp.dot(jnp.concatenate(chosen, axis=1), tall, preferred_element_type=F32)


def yd_kernel(at, y_pairs, d_pairs, fetched, z, d, s_in, zt_in, y, sems):
    count = fetched.shape[0]
    columns, slots, size = z.shape[:3]
    copies = [
        pltpu.make_async_copy(fetched.at[:, i], into.at[pl.ds(0, count)], sems.at[i])
        for i, into in zip(at, (s_in, zt_in))
    ]
    for copy in copies:
        copy.start()
    s_in[count] = jnp.zeros((size, size), BF16)
    zt_in[count] = jnp.zeros((size, size), BF16)
    copies[0].wait()
    for g in range(columns):
        for a in range(slots):
            y[g, a] = product(y_pairs, s_in, g, a, z[g]).astype(BF16)
    copies[1].wait()

    @pl.loop(0, count)
    def _(i):
        zt_in[i] = zt_in[i].T

    rows = lax.broadcasted_iota(jnp.int32, (size, size), 0)
    identity = jnp.where(rows == lax.broadcasted_iota(jnp.int32, (size, size), 1), 1.0, 0.0)
    for g in range(columns):
        for a in range(slots):
            total = product(d_pairs, zt_in, g, a, y[g])
            d[g, a] = (identity - total if a == 0 else -total).astype(BF16)


def ez_kernel(at, e_pairs, z_pairs, d_fetched, z_fetched, d, z, out, d_in, z_in, e, sems):
    count = d_fetched.shape[0]
    columns, slots, size = z.shape[:3]
    copies = [
        pltpu.make_async_copy(src.at[:, i], into.at[pl.ds(0, count)], sems.at[k])
        for k, (i, src, into) in enumerate(zip(at, (d_fetched, z_fetched), (d_in, z_in)))
    ]
    for copy in copies:
        copy.start()
    d_in[count] = jnp.zeros((size, size), BF16)
    z_in[count] = jnp.zeros((size, size), BF16)
    copies[0].wait()
    for g in range(columns):
        for a in range(slots):
            square = product(e_pairs, d_in, g, a, d[g])
            e[g, a] = (0.5 * d[g, a].astype(F32) + 0.375 * square).astype(BF16)
    copies[1].wait()
    for g in range(columns):
        for a in range(slots):
            total = z[g, a].astype(F32) + product(z_pairs, z_in, g, a, e[g])
            out[g, a] = total.astype(BF16)


def paired_call(body, name, pairs, fetched, local):
    columns, slots, size = local[0].shape[:3]
    count = fetched[0].shape[0]
    flops = 4 * columns * slots * slots * size**3
    return pl.pallas_call(
        body,
        out_shape=jax.ShapeDtypeStruct(local[0].shape, BF16),
        in_specs=[SMEM] * 2 + [ANY] * len(fetched) + [VMEM] * len(local),
        out_specs=VMEM,
        scratch_shapes=[
            pltpu.VMEM((count + 1, size, size), BF16),
            pltpu.VMEM((count + 1, size, size), BF16),
            pltpu.VMEM(local[0].shape, BF16),
            pltpu.SemaphoreType.DMA((2,)),
        ],
        compiler_params=pltpu.CompilerParams(vmem_limit_bytes=32 * 2**20),
        cost_estimate=pl.CostEstimate(flops=flops, bytes_accessed=16 * 2**20, transcendentals=0),
        name=name,
    )(*pairs, *fetched, *local)


def on_device(
    s_blocks, z_blocks, s_requests, y_pairs, zt_requests, d_pairs, d_requests, e_pairs, z_requests, z_pairs
):
    flat_shape = (-1,) + z_blocks.shape[2:]
    peers = s_requests.shape[2]
    wanted = [r.reshape(peers, 1) for r in (s_requests, zt_requests, z_requests, d_requests)]
    asks = exchange(jnp.concatenate(wanted, axis=1))
    s_own = s_blocks.reshape(flat_shape)
    z_own = z_blocks.reshape(flat_shape)
    z_other = from_partner(z_own)
    first = pick(asks, (s_own, z_own, z_other), ((0, 0, 1), (1, 1, 3)), "pick_s_zt")
    second = pick(asks, (z_own, z_other), ((2, 0, 2),), "pick_z")
    first = exchange(first)
    first, second = lax.optimization_barrier((first, second))
    z_fetched = exchange(second)
    make_d = functools.partial(yd_kernel, (0, 1))
    d_blocks = paired_call(make_d, "make_d", (y_pairs, d_pairs), (first,), (z_blocks,))
    d_own = d_blocks.reshape(flat_shape)
    d_other = from_partner(d_own)
    third = pick(asks, (d_own, d_other), ((3, 0, 2),), "pick_d")
    d_fetched = exchange(third)
    refine = functools.partial(ez_kernel, (0, 0))
    return paired_call(refine, "refine", (e_pairs, z_pairs), (d_fetched, z_fetched), (d_blocks, z_blocks))


def solution(mesh):
    blocks = P(("leaf", "col"), None, None, None)
    requests = P("leaf", "col", None, None)
    pairs = P(("leaf", "col"), None, None)
    in_specs = (blocks, blocks) + (requests, pairs) * 4
    return jax.shard_map(on_device, mesh=mesh, in_specs=in_specs, out_specs=blocks, check_vma=False)
```

time: 271 us -> 268 us (0.989)
  Pallas kernels: 25.4 us -> 17.2 us
  waiting for transfers between devices: 137 us -> 142 us
    pallas_call x2, Pallas kernels: 18.2 us -> 9.98 us  [paired_call(): pl.pallas_call(body, out_shape=jax.ShapeDtypeStruct(local[0].shape, BF16)...]
    all_to_all x2, waiting for transfers between devices: 124 us -> 129 us  [exchange(): return lax.all_to_all(value, 'col', split_axis=0, concat_axis=0, tiled=True)]
  transfers between devices with their start and end apart: 4 -> 4, of which waited for: 3 -> 3; matrix products, arithmetic and copies ran while one was open for 0% -> 0% of each run, Pallas kernels for 5% -> 4%
where the time goes in v2:
time: 268 us; the launch traced here: 267 us
  waiting for transfers between devices  142 us (53%)
  blocking collectives  88.3 us (33%)
  starting transfers between devices  17.4 us (6%)
  Pallas kernels  17.2 us (6%)
    all_to_all x2, waiting for transfers between devices, exchange(): return lax.all_to_all(value, 'col', split_axis=0, concat_axis=0, tiled=True)  129 us
    all_to_all x2, blocking collectives, exchange(): return lax.all_to_all(value, 'col', split_axis=0, concat_axis=0, tiled=True)  88.3 us
    ppermute x2, waiting for transfers between devices, from_partner(): return lax.ppermute(value, 'leaf', pairs)  13 us
    all_to_all x2, starting transfers between devices, exchange(): return lax.all_to_all(value, 'col', split_axis=0, concat_axis=0, tiled=True)  11.2 us
    pallas_call x2, Pallas kernels, paired_call(): pl.pallas_call(body, out_shape=jax.ShapeDtypeStruct(local[0].shape, BF16)...  9.98 us
    pallas_call x3, Pallas kernels, pick(): pl.pallas_call(functools.partial(pick_kernel, lists), out_shape=jax.Shape...  7.22 us
    ppermute x2, starting transfers between devices, from_partner(): return lax.ppermute(value, 'leaf', pairs)  6.23 us
  transfers between devices with their start and end apart: 4, of which 3 were waited for; matrix products, arithmetic and copies ran while one was open for 0% of the time, Pallas kernels for 4%

profile of v2, /device:TPU:1, one launch (start us, length us, event | category | flops | bytes accessed | tf_op | source)
XLA Modules:
  0.0 267.3 jit_solution(5591313425436664755)
XLA Ops:
  0.0 4.0 %collective-permute-start = (bf16[16,128,128]{2,1,0:T(8,128)(2,1)}, bf16[16,128,128]{2,1,0:T(8,128)(2,1)S(1)}, u32[]{:S(2)}, u32[]{:S(2)}) collective-permute-start(bf16[16,128,128]{2,1,0:T(8,128)(2,1)} %bitcast.10), channel_id=1, source_target_pairs={{0,32},{32,0},{64,96},{96,64},{128,160},{160,128},{192,224},{224,1... | collective-permute-start | bytes 1572872 | tf_op jit(solution)/shard_map/ppermute | solution.py:19
  4.0 0.7 add_bitcast_fusion
  4.7 0.1 copy.14
  4.8 27.9 %all_to_all.26 = s32[32,1,4]{2,1,0:T(1,128)} all-to-all(s32[32,1,4]{2,1,0:T(1,128)S(1)} %copy.14), channel_id=1, replica_groups=mesh['leaf'=16,'col'=32] {'col'}, dimensions={0} | all-to-all | bytes 1024 | tf_op jit(solution)/shard_map/all_to_all | solution.py:23
  32.7 0.0 collective-permute-done.refs_2_.refs_1_
  32.7 0.8 copy-done.7
  33.5 2.7 %pick_s_zt.1 = bf16[32,2,128,128]{3,2,1,0:T(8,128)(2,1)} custom-call(s32[32,4]{1,0:T(8,128)} %bitcast.16, bf16[16,128,128]{2,1,0:T(8,128)(2,1)} %bitcast.15, bf16[16,128,128]{2,1,0:T(8,128)(2,1)} %bitcast.11, bf16[16,128,128]{2,1,0:T(8,128)(2,1)} %copy-done.7), custom_call_target="tpu_custom_call" | custom-call | bytes 6291456 | tf_op jit(solution)/shard_map/pick_s_zt/pallas_call | solution.py:66
  36.3 4.4 %all-to-all-start.1 = ((bf16[32,2,128,128]{3,2,1,0:T(8,128)(2,1)}), bf16[32,2,128,128]{3,2,1,0:T(8,128)(2,1)S(1)}, u32[]{:S(2)}, u32[]{:S(2)}) async-start(bf16[32,2,128,128]{3,2,1,0:T(8,128)(2,1)} %pick_s_zt.1), calls=%async_computation.1 | async-start | bytes 4194304 | tf_op jit(solution)/shard_map/all_to_all | solution.py:23
  40.7 0.0 copy-start
  40.7 0.0 copy-start.3
  40.7 0.0 copy-start.4
  40.7 2.3 pick_z.1
  43.0 97.0 %all-to-all-done.1.fetched = bf16[32,2,128,128]{3,2,1,0:T(8,128)(2,1)S(1)} async-done(((bf16[32,2,128,128]{3,2,1,0:T(8,128)(2,1)}), bf16[32,2,128,128]{3,2,1,0:T(8,128)(2,1)S(1)}, u32[]{:S(2)}, u32[]{:S(2)}) %all-to-all-start.1) | async-done | bytes 2097184 | tf_op jit(solution)/shard_map/all_to_all | solution.py:23
  140.0 6.7 %all-to-all-start.3 = ((bf16[32,1,128,128]{3,2,1,0:T(8,128)(2,1)}), bf16[32,1,128,128]{3,2,1,0:T(8,128)(2,1)}, u32[]{:S(2)}, u32[]{:S(2)}) async-start(bf16[32,1,128,128]{3,2,1,0:T(8,128)(2,1)} %pick_z.1), calls=%async_computation.3 | async-start | bytes 2097152 | tf_op jit(solution)/shard_map/all_to_all | solution.py:23
  146.8 0.0 copy-done
  146.8 0.0 copy-done.3
  146.8 0.0 copy-done.4
  146.8 5.7 %make_d.1.d = bf16[2,8,128,128]{3,2,1,0:T(8,128)(2,1)S(1)} custom-call(s32[2,8,8]{2,1,0:T(8,128)S(1)} %copy-done.3, s32[2,8,8]{2,1,0:T(8,128)S(1)} %copy-done.4, bf16[32,2,128,128]{3,2,1,0:T(8,128)(2,1)S(1)} %all-to-all-done.1.fetched, bf16[2,8,128,128]{3,2,1,0:T(8,128)(2,1)S(1)} %copy-done), custom_call_target="tpu_custom_call" | custom-call | flops 1073741824 | bytes 16777216 | tf_op jit(solution)/shard_map/make_d/pallas_call | solution.py:148
  152.5 0.0 copy-start.1
  152.5 0.0 copy-start.5
  152.6 0.0 copy-start.6
  152.6 2.2 collective-permute-start.1
  154.8 13.0 %collective-permute-done.1.refs_1_ = bf16[16,128,128]{2,1,0:T(8,128)(2,1)S(1)} collective-permute-done((bf16[16,128,128]{2,1,0:T(8,128)(2,1)S(1)}, bf16[16,128,128]{2,1,0:T(8,128)(2,1)S(1)}, u32[]{:S(2)}, u32[]{:S(2)}) %collective-permute-start.1) | collective-permute-done | bytes 524320 | tf_op jit(solution)/shard_map/ppermute | solution.py:19
  167.8 0.0 copy-done.1
  167.8 0.8 copy-done.8
  168.6 2.2 pick_d.1
  170.8 0.0 copy-start.2
  170.8 31.8 %all-to-all-done.3.z_fetched = bf16[32,1,128,128]{3,2,1,0:T(8,128)(2,1)} async-done(((bf16[32,1,128,128]{3,2,1,0:T(8,128)(2,1)}), bf16[32,1,128,128]{3,2,1,0:T(8,128)(2,1)}, u32[]{:S(2)}, u32[]{:S(2)}) %all-to-all-start.3) | async-done | bytes 1048608 | tf_op jit(solution)/shard_map/all_to_all | solution.py:23
  202.6 60.4 %all_to_all.27.d_fetched = bf16[32,1,128,128]{3,2,1,0:T(8,128)(2,1)S(1)} all-to-all(bf16[32,1,128,128]{3,2,1,0:T(8,128)(2,1)} %pick_d.1), channel_id=1, replica_groups=mesh['leaf'=16,'col'=32] {'col'}, dimensions={0} | all-to-all | bytes 2097152 | tf_op jit(solution)/shard_map/all_to_all | solution.py:23
  263.1 0.0 copy-done.5
  263.1 0.0 copy-done.6
  263.1 4.3 %refine.1 = bf16[2,8,128,128]{3,2,1,0:T(8,128)(2,1)} custom-call(s32[2,8,8]{2,1,0:T(8,128)S(1)} %copy-done.5, s32[2,8,8]{2,1,0:T(8,128)S(1)} %copy-done.6, bf16[32,1,128,128]{3,2,1,0:T(8,128)(2,1)S(1)} %all_to_all.27.d_fetched, bf16[32,1,128,128]{3,2,1,0:T(8,128)(2,1)} %all-to-all-done.3.z_fetched, bf16[2,8,128,128]{3,2,1,0:T(8,128)(2,1)S(1)} %copy-done.2, ...), custom_call_target="tpu_custom_call" | custom-call | flops 1073741824 | bytes 16777216 | tf_op jit(solution)/shard_map/refine/pallas_call | solution.py:148
  (3 shorter events, 0.0 us)
Async XLA Ops:
  0.0 32.7 %collective-permute-start = (bf16[16,128,128]{2,1,0:T(8,128)(2,1)}, bf16[16,128,128]{2,1,0:T(8,128)(2,1)S(1)}, u32[]{:S(2)}, u32[]{:S(2)}) collective-permute-start(bf16[16,128,128]{2,1,0:T(8,128)(2,1)} %bitcast.10), channel_id=1, source_target_pairs={{0,32},{32,0},{64,96},{96,64},{128,160},{160,128},{192,224},{224,1... | collective-permute-start | bytes 1572872 | tf_op jit(solution)/shard_map/ppermute | solution.py:19
  32.7 0.8 copy-start.7
  36.3 103.7 %all-to-all-start.1 = ((bf16[32,2,128,128]{3,2,1,0:T(8,128)(2,1)}), bf16[32,2,128,128]{3,2,1,0:T(8,128)(2,1)S(1)}, u32[]{:S(2)}, u32[]{:S(2)}) async-start(bf16[32,2,128,128]{3,2,1,0:T(8,128)(2,1)} %pick_s_zt.1), calls=%async_computation.1 | async-start | bytes 4194304 | tf_op jit(solution)/shard_map/all_to_all | solution.py:23
  40.7 106.1 %copy-start = (bf16[2,8,128,128]{3,2,1,0:T(8,128)(2,1)S(1)}, bf16[2,8,128,128]{3,2,1,0:T(8,128)(2,1)}, u32[]{:S(2)}) copy-start(bf16[2,8,128,128]{3,2,1,0:T(8,128)(2,1)} %z.3) | copy-start | bytes 1572868
  40.7 106.1 %copy-start.3 = (s32[2,8,8]{2,1,0:T(8,128)S(1)}, s32[2,8,8]{2,1,0:T(8,128)}, u32[]{:S(2)}) copy-start(s32[2,8,8]{2,1,0:T(8,128)} %y_pairs.1) | copy-start | bytes 1540
  40.7 106.0 %copy-start.4 = (s32[2,8,8]{2,1,0:T(8,128)S(1)}, s32[2,8,8]{2,1,0:T(8,128)}, u32[]{:S(2)}) copy-start(s32[2,8,8]{2,1,0:T(8,128)} %d_pairs.1) | copy-start | bytes 1540
  140.0 62.6 %all-to-all-start.3 = ((bf16[32,1,128,128]{3,2,1,0:T(8,128)(2,1)}), bf16[32,1,128,128]{3,2,1,0:T(8,128)(2,1)}, u32[]{:S(2)}, u32[]{:S(2)}) async-start(bf16[32,1,128,128]{3,2,1,0:T(8,128)(2,1)} %pick_z.1), calls=%async_computation.3 | async-start | bytes 2097152 | tf_op jit(solution)/shard_map/all_to_all | solution.py:23
  152.5 15.2 %copy-start.1 = (bf16[2,8,128,128]{3,2,1,0:T(8,128)(2,1)}, bf16[2,8,128,128]{3,2,1,0:T(8,128)(2,1)S(1)}, u32[]{:S(2)}) copy-start(bf16[2,8,128,128]{3,2,1,0:T(8,128)(2,1)S(1)} %make_d.1.d) | copy-start | bytes 1572868
  152.5 110.5 %copy-start.5 = (s32[2,8,8]{2,1,0:T(8,128)S(1)}, s32[2,8,8]{2,1,0:T(8,128)}, u32[]{:S(2)}) copy-start(s32[2,8,8]{2,1,0:T(8,128)} %e_pairs.1) | copy-start | bytes 1540
  152.6 110.5 %copy-start.6 = (s32[2,8,8]{2,1,0:T(8,128)S(1)}, s32[2,8,8]{2,1,0:T(8,128)}, u32[]{:S(2)}) copy-start(s32[2,8,8]{2,1,0:T(8,128)} %z_pairs.1) | copy-start | bytes 1540
  152.6 15.2 %collective-permute-start.1 = (bf16[16,128,128]{2,1,0:T(8,128)(2,1)S(1)}, bf16[16,128,128]{2,1,0:T(8,128)(2,1)S(1)}, u32[]{:S(2)}, u32[]{:S(2)}) collective-permute-start(bf16[16,128,128]{2,1,0:T(8,128)(2,1)S(1)} %bitcast.13), channel_id=1, source_target_pairs={{0,32},{32,0},{64,96},{96,64},{128,160},{160,128},{192,224},{224,1... | collective-permute-start | bytes 1572872 | tf_op jit(solution)/shard_map/ppermute | solution.py:19
  167.8 0.8 copy-start.8
  170.8 92.2 %copy-start.2 = (bf16[2,8,128,128]{3,2,1,0:T(8,128)(2,1)S(1)}, bf16[2,8,128,128]{3,2,1,0:T(8,128)(2,1)}, u32[]{:S(2)}) copy-start(bf16[2,8,128,128]{3,2,1,0:T(8,128)(2,1)} %copy-done.1) | copy-start | bytes 1572868

commit v3 on v2

--- a/solution.py
+++ b/solution.py
@@ -19,8 +19,25 @@
     return lax.ppermute(value, "leaf", pairs)
 
 
+def standing(peer, count):
+    return (count // 2 + 1 - peer + count) % count
+
+
 def exchange(value):
-    return lax.all_to_all(value, "col", split_axis=0, concat_axis=0, tiled=True)
+    count = lax.axis_size("col")
+    group = sorted(range(count), key=lambda peer: standing(peer, count))
+    return lax.all_to_all(value, "col", 0, 0, axis_index_groups=[group], tiled=True)
+
+
+def exchange_asks(asks):
+    count = asks.shape[0]
+    group = [(row + count // 2) % count for row in range(count)]
+    asks = jnp.roll(asks, -(count // 2), axis=0)
+    return lax.all_to_all(asks, "col", 0, 0, axis_index_groups=[group], tiled=True)
+
+
+def asks_row(place, count):
+    return lax.rem(count + 1 - place, count)
 
 
 def pick_kernel(lists, asks, *refs):
@@ -49,7 +66,7 @@
     @pl.loop(0, readers)
     def _(reader):
         for place, (store, size, (row, _, _)) in enumerate(zip(stores, sizes, lists)):
-            slot = asked[reader, row]
+            slot = asked[asks_row(reader, readers), row]
             at = jnp.where(slot < 0, size, slot)
             pltpu.make_async_copy(store.at[at], out.at[reader, place], sem).start()
 
@@ -80,11 +97,7 @@
 
 
 def product(pairs, blocks, g, a, right):
-    slots, last = pairs.shape[2], blocks.shape[0] - 1
-    chosen = []
-    for b in range(slots):
-        pair = pairs[g, a, b]
-        chosen.append(blocks[jnp.where(pair < 0, last, pair)])
+    chosen = [blocks[pairs[g, a, b]] for b in range(pairs.shape[2])]
     tall = right.reshape(right.shape[0] * right.shape[1], right.shape[2])
     return jnp.dot(jnp.concatenate(chosen, axis=1), tall, preferred_element_type=F32)
 
@@ -168,7 +181,10 @@
     flat_shape = (-1,) + z_blocks.shape[2:]
     peers = s_requests.shape[2]
     wanted = [r.reshape(peers, 1) for r in (s_requests, zt_requests, z_requests, d_requests)]
-    asks = exchange(jnp.concatenate(wanted, axis=1))
+    asks = exchange_asks(jnp.concatenate(wanted, axis=1))
+    pairs = [
+        jnp.where(pair < 0, peers, standing(jnp.maximum(pair, 0), peers)) for pair in (y_pairs, d_pairs, e_pairs, z_pairs)
+    ]
     s_own = s_blocks.reshape(flat_shape)
     z_own = z_blocks.reshape(flat_shape)
     z_other = from_partner(z_own)
@@ -178,13 +194,13 @@
     first, second = lax.optimization_barrier((first, second))
     z_fetched = exchange(second)
     make_d = functools.partial(yd_kernel, (0, 1))
-    d_blocks = paired_call(make_d, "make_d", (y_pairs, d_pairs), (first,), (z_blocks,))
+    d_blocks = paired_call(make_d, "make_d", pairs[:2], (first,), (z_blocks,))
     d_own = d_blocks.reshape(flat_shape)
     d_other = from_partner(d_own)
     third = pick(asks, (d_own, d_other), ((3, 0, 2),), "pick_d")
     d_fetched = exchange(third)
     refine = functools.partial(ez_kernel, (0, 0))
-    return paired_call(refine, "refine", (e_pairs, z_pairs), (d_fetched, z_fetched), (d_blocks, z_blocks))
+    return paired_call(refine, "refine", pairs[2:], (d_fetched, z_fetched), (d_blocks, z_blocks))
 
 
 def solution(mesh):

time: 268 us -> 256 us (0.955)
  blocking collectives: 88.3 us -> 21.7 us
  starting transfers between devices: 17.4 us -> 44.6 us
  waiting for transfers between devices: 142 us -> 169 us
    all_to_all x2 -> x1, blocking collectives: 88.3 us -> 21.7 us  [exchange_asks(): lax.all_to_all(asks, 'col', 0, 0, axis_index_groups=[group], tiled=True)]
    all_to_all x2 -> x3, waiting for transfers between devices: 129 us -> 157 us  [exchange(): lax.all_to_all(value, 'col', 0, 0, axis_index_groups=[group], tiled=True)]
    all_to_all x2 -> x3, starting transfers between devices: 11.2 us -> 38.4 us  [exchange(): lax.all_to_all(value, 'col', 0, 0, axis_index_groups=[group], tiled=True)]
  transfers between devices with their start and end apart: 4 -> 5, of which waited for: 3 -> 4; matrix products, arithmetic and copies ran while one was open for 0% -> 0% of each run, Pallas kernels for 4% -> 4%
where the time goes in v3:
time: 256 us
  waiting for transfers between devices  169 us (66%)
  starting transfers between devices  44.6 us (17%)
  blocking collectives  21.7 us (8%)
  Pallas kernels  17.1 us (7%)
    all_to_all x3, waiting for transfers between devices, exchange(): lax.all_to_all(value, 'col', 0, 0, axis_index_groups=[group], tiled=True)  157 us
    all_to_all x3, starting transfers between devices, exchange(): lax.all_to_all(value, 'col', 0, 0, axis_index_groups=[group], tiled=True)  38.4 us
    all_to_all x1, blocking collectives, exchange_asks(): lax.all_to_all(asks, 'col', 0, 0, axis_index_groups=[group], tiled=True)  21.7 us
    ppermute x2, waiting for transfers between devices, from_partner(): return lax.ppermute(value, 'leaf', pairs)  13 us
    pallas_call x2, Pallas kernels, paired_call(): pl.pallas_call(body, out_shape=jax.ShapeDtypeStruct(local[0].shape, BF16)...  9.93 us
    pallas_call x3, Pallas kernels, pick(): pl.pallas_call(functools.partial(pick_kernel, lists), out_shape=jax.Shape...  7.22 us
    ppermute x2, starting transfers between devices, from_partner(): return lax.ppermute(value, 'leaf', pairs)  6.23 us
  transfers between devices with their start and end apart: 5, of which 4 were waited for; matrix products, arithmetic and copies ran while one was open for 0% of the time, Pallas kernels for 4%

profile of v3, /device:TPU:1, one launch (start us, length us, event | category | flops | bytes accessed | tf_op | source)
XLA Modules:
  0.0 255.7 jit_solution(18051083458285189801)
XLA Ops:
  0.0 4.0 %collective-permute-start = (bf16[16,128,128]{2,1,0:T(8,128)(2,1)}, bf16[16,128,128]{2,1,0:T(8,128)(2,1)S(1)}, u32[]{:S(2)}, u32[]{:S(2)}) collective-permute-start(bf16[16,128,128]{2,1,0:T(8,128)(2,1)} %bitcast.10), channel_id=1, source_target_pairs={{0,32},{32,0},{64,96},{96,64},{128,160},{160,128},{192,224},{224,1... | collective-permute-start | bytes 1572872 | tf_op jit(solution)/shard_map/ppermute | solution.py:19
  4.0 0.7 pad_add_fusion
  4.7 0.1 fusion.8
  4.8 0.1 add_bitcast_fusion
  4.9 0.1 copy.14
  5.0 21.7 %all_to_all.26 = s32[32,1,4]{2,1,0:T(1,128)} all-to-all(s32[32,1,4]{2,1,0:T(1,128)S(1)} %copy.14), channel_id=1, replica_groups={{16,17,18,19,20,21,22,23,24,25,26,27,28,29,30,31,0,1,2,3,4,5,6,7,8,9,10..., dimensions={0} | all-to-all | bytes 1024 | tf_op jit(solution)/shard_map/all_to_all | solution.py:36
  26.7 0.0 collective-permute-done.refs_2_.refs_1_
  26.7 0.8 copy-done.3
  27.5 2.7 %pick_s_zt.1 = bf16[32,2,128,128]{3,2,1,0:T(8,128)(2,1)} custom-call(s32[32,4]{1,0:T(8,128)} %bitcast.16, bf16[16,128,128]{2,1,0:T(8,128)(2,1)} %bitcast.15, bf16[16,128,128]{2,1,0:T(8,128)(2,1)} %bitcast.11, bf16[16,128,128]{2,1,0:T(8,128)(2,1)} %copy-done.3), custom_call_target="tpu_custom_call" | custom-call | bytes 6291456 | tf_op jit(solution)/shard_map/pick_s_zt/pallas_call | solution.py:83
  30.2 13.5 %all-to-all-start.1 = ((bf16[32,2,128,128]{3,2,1,0:T(8,128)(2,1)}), bf16[32,2,128,128]{3,2,1,0:T(8,128)(2,1)S(1)}, u32[]{:S(2)}, u32[]{:S(2)}) async-start(bf16[32,2,128,128]{3,2,1,0:T(8,128)(2,1)} %pick_s_zt.1), calls=%async_computation.1 | async-start | bytes 4194304 | tf_op jit(solution)/shard_map/all_to_all | solution.py:29
  43.7 0.0 copy-start.5
  43.7 0.0 copy-start.6
  43.7 0.0 copy-start
  43.7 2.3 pick_z.1
  46.0 88.9 %all-to-all-done.1.fetched = bf16[32,2,128,128]{3,2,1,0:T(8,128)(2,1)S(1)} async-done(((bf16[32,2,128,128]{3,2,1,0:T(8,128)(2,1)}), bf16[32,2,128,128]{3,2,1,0:T(8,128)(2,1)S(1)}, u32[]{:S(2)}, u32[]{:S(2)}) %all-to-all-start.1) | async-done | bytes 2097184 | tf_op jit(solution)/shard_map/all_to_all | solution.py:29
  134.9 12.3 %all-to-all-start.3 = ((bf16[32,1,128,128]{3,2,1,0:T(8,128)(2,1)}), bf16[32,1,128,128]{3,2,1,0:T(8,128)(2,1)}, u32[]{:S(2)}, u32[]{:S(2)}) async-start(bf16[32,1,128,128]{3,2,1,0:T(8,128)(2,1)} %pick_z.1), calls=%async_computation.3 | async-start | bytes 2097152 | tf_op jit(solution)/shard_map/all_to_all | solution.py:29
  147.2 0.0 copy-done.5
  147.2 0.0 copy-done.6
  147.2 0.0 copy-done
  147.2 5.7 %make_d.1.d = bf16[2,8,128,128]{3,2,1,0:T(8,128)(2,1)S(1)} custom-call(s32[2,8,8]{2,1,0:T(8,128)S(1)} %get-tuple-element.11.y_pairs, s32[2,8,8]{2,1,0:T(8,128)S(1)} %get-tuple-element.12.d_pairs, bf16[32,2,128,128]{3,2,1,0:T(8,128)(2,1)S(1)} %all-to-all-done.1.fetched, bf16[2,8,128,128]{3,2,1,0:T(8,128)(2,1)S(1)} %copy-done), custom_call_target="tpu_custom_call" | custom-call | flops 1073741824 | bytes 16777216 | tf_op jit(solution)/shard_map/make_d/pallas_call | solution.py:161
  153.0 0.0 copy-start.1
  153.0 0.0 copy-start.7
  153.0 0.0 copy-start.8
  153.0 2.2 collective-permute-start.1
  155.2 13.0 %collective-permute-done.1.refs_1_ = bf16[16,128,128]{2,1,0:T(8,128)(2,1)S(1)} collective-permute-done((bf16[16,128,128]{2,1,0:T(8,128)(2,1)S(1)}, bf16[16,128,128]{2,1,0:T(8,128)(2,1)S(1)}, u32[]{:S(2)}, u32[]{:S(2)}) %collective-permute-start.1) | collective-permute-done | bytes 524320 | tf_op jit(solution)/shard_map/ppermute | solution.py:19
  168.2 0.8 copy-done.4
  169.0 2.2 pick_d.1
  171.2 0.0 copy-start.2
  171.2 21.8 %all-to-all-done.3.z_fetched = bf16[32,1,128,128]{3,2,1,0:T(8,128)(2,1)} async-done(((bf16[32,1,128,128]{3,2,1,0:T(8,128)(2,1)}), bf16[32,1,128,128]{3,2,1,0:T(8,128)(2,1)}, u32[]{:S(2)}, u32[]{:S(2)}) %all-to-all-start.3) | async-done | bytes 1048608 | tf_op jit(solution)/shard_map/all_to_all | solution.py:29
  193.1 12.6 %all-to-all-start.2 = ((bf16[32,1,128,128]{3,2,1,0:T(8,128)(2,1)}), bf16[32,1,128,128]{3,2,1,0:T(8,128)(2,1)S(1)}, u32[]{:S(2)}, u32[]{:S(2)}) async-start(bf16[32,1,128,128]{3,2,1,0:T(8,128)(2,1)} %pick_d.1), calls=%async_computation.2 | async-start | bytes 2097152 | tf_op jit(solution)/shard_map/all_to_all | solution.py:29
  205.7 45.8 %all-to-all-done.2.d_fetched = bf16[32,1,128,128]{3,2,1,0:T(8,128)(2,1)S(1)} async-done(((bf16[32,1,128,128]{3,2,1,0:T(8,128)(2,1)}), bf16[32,1,128,128]{3,2,1,0:T(8,128)(2,1)S(1)}, u32[]{:S(2)}, u32[]{:S(2)}) %all-to-all-start.2) | async-done | bytes 1048608 | tf_op jit(solution)/shard_map/all_to_all | solution.py:29
  251.5 4.2 %refine.1 = bf16[2,8,128,128]{3,2,1,0:T(8,128)(2,1)} custom-call(s32[2,8,8]{2,1,0:T(8,128)S(1)} %get-tuple-element.13.e_pairs, s32[2,8,8]{2,1,0:T(8,128)S(1)} %get-tuple-element.14.z_pairs, bf16[32,1,128,128]{3,2,1,0:T(8,128)(2,1)S(1)} %all-to-all-done.2.d_fetched, bf16[32,1,128,128]{3,2,1,0:T(8,128)(2,1)} %all-to-all-done.3.z_fetched, ...), custom_call_target="tpu_custom_call" | custom-call | flops 1073741824 | bytes 16777216 | tf_op jit(solution)/shard_map/refine/pallas_call | solution.py:161
  (8 shorter events, 0.0 us)
Async XLA Ops:
  0.0 26.7 %collective-permute-start = (bf16[16,128,128]{2,1,0:T(8,128)(2,1)}, bf16[16,128,128]{2,1,0:T(8,128)(2,1)S(1)}, u32[]{:S(2)}, u32[]{:S(2)}) collective-permute-start(bf16[16,128,128]{2,1,0:T(8,128)(2,1)} %bitcast.10), channel_id=1, source_target_pairs={{0,32},{32,0},{64,96},{96,64},{128,160},{160,128},{192,224},{224,1... | collective-permute-start | bytes 1572872 | tf_op jit(solution)/shard_map/ppermute | solution.py:19
  26.7 0.8 copy-start.3
  30.2 104.7 %all-to-all-start.1 = ((bf16[32,2,128,128]{3,2,1,0:T(8,128)(2,1)}), bf16[32,2,128,128]{3,2,1,0:T(8,128)(2,1)S(1)}, u32[]{:S(2)}, u32[]{:S(2)}) async-start(bf16[32,2,128,128]{3,2,1,0:T(8,128)(2,1)} %pick_s_zt.1), calls=%async_computation.1 | async-start | bytes 4194304 | tf_op jit(solution)/shard_map/all_to_all | solution.py:29
  43.7 103.5 %copy-start.5 = (s32[2,8,8]{2,1,0:T(8,128)S(1)}, s32[2,8,8]{2,1,0:T(8,128)}, u32[]{:S(2)}) copy-start(s32[2,8,8]{2,1,0:T(8,128)} %param.13) | copy-start | bytes 1540
  43.7 103.5 %copy-start.6 = (s32[2,8,8]{2,1,0:T(8,128)S(1)}, s32[2,8,8]{2,1,0:T(8,128)}, u32[]{:S(2)}) copy-start(s32[2,8,8]{2,1,0:T(8,128)} %param.15) | copy-start | bytes 1540
  43.7 103.5 %copy-start = (bf16[2,8,128,128]{3,2,1,0:T(8,128)(2,1)S(1)}, bf16[2,8,128,128]{3,2,1,0:T(8,128)(2,1)}, u32[]{:S(2)}) copy-start(bf16[2,8,128,128]{3,2,1,0:T(8,128)(2,1)} %z.3) | copy-start | bytes 1572868
  134.9 58.2 %all-to-all-start.3 = ((bf16[32,1,128,128]{3,2,1,0:T(8,128)(2,1)}), bf16[32,1,128,128]{3,2,1,0:T(8,128)(2,1)}, u32[]{:S(2)}, u32[]{:S(2)}) async-start(bf16[32,1,128,128]{3,2,1,0:T(8,128)(2,1)} %pick_z.1), calls=%async_computation.3 | async-start | bytes 2097152 | tf_op jit(solution)/shard_map/all_to_all | solution.py:29
  153.0 15.2 %copy-start.1 = (bf16[2,8,128,128]{3,2,1,0:T(8,128)(2,1)}, bf16[2,8,128,128]{3,2,1,0:T(8,128)(2,1)S(1)}, u32[]{:S(2)}) copy-start(bf16[2,8,128,128]{3,2,1,0:T(8,128)(2,1)S(1)} %make_d.1.d) | copy-start | bytes 1572868
  153.0 52.7 %copy-start.7 = (s32[2,8,8]{2,1,0:T(8,128)S(1)}, s32[2,8,8]{2,1,0:T(8,128)}, u32[]{:S(2)}) copy-start(s32[2,8,8]{2,1,0:T(8,128)} %param.17) | copy-start | bytes 1540
  153.0 52.7 %copy-start.8 = (s32[2,8,8]{2,1,0:T(8,128)S(1)}, s32[2,8,8]{2,1,0:T(8,128)}, u32[]{:S(2)}) copy-start(s32[2,8,8]{2,1,0:T(8,128)} %param.19) | copy-start | bytes 1540
  153.0 15.2 %collective-permute-start.1 = (bf16[16,128,128]{2,1,0:T(8,128)(2,1)S(1)}, bf16[16,128,128]{2,1,0:T(8,128)(2,1)S(1)}, u32[]{:S(2)}, u32[]{:S(2)}) collective-permute-start(bf16[16,128,128]{2,1,0:T(8,128)(2,1)S(1)} %bitcast.13), channel_id=1, source_target_pairs={{0,32},{32,0},{64,96},{96,64},{128,160},{160,128},{192,224},{224,1... | collective-permute-start | bytes 1572872 | tf_op jit(solution)/shard_map/ppermute | solution.py:19
  168.2 0.8 copy-start.4
  171.2 80.3 %copy-start.2 = (bf16[2,8,128,128]{3,2,1,0:T(8,128)(2,1)S(1)}, bf16[2,8,128,128]{3,2,1,0:T(8,128)(2,1)}, u32[]{:S(2)}) copy-start(bf16[2,8,128,128]{3,2,1,0:T(8,128)(2,1)} %copy-done.1) | copy-start | bytes 1572868
  193.1 58.5 %all-to-all-start.2 = ((bf16[32,1,128,128]{3,2,1,0:T(8,128)(2,1)}), bf16[32,1,128,128]{3,2,1,0:T(8,128)(2,1)S(1)}, u32[]{:S(2)}, u32[]{:S(2)}) async-start(bf16[32,1,128,128]{3,2,1,0:T(8,128)(2,1)} %pick_d.1), calls=%async_computation.2 | async-start | bytes 2097152 | tf_op jit(solution)/shard_map/all_to_all | solution.py:29

commit v4 on v3

--- a/solution.py
+++ b/solution.py
@@ -19,8 +19,12 @@
     return lax.ppermute(value, "leaf", pairs)
 
 
+def first_of(count):
+    return count // 2 + 1
+
+
 def standing(peer, count):
-    return (count // 2 + 1 - peer + count) % count
+    return (first_of(count) - peer + count) % count
 
 
 def exchange(value):
@@ -29,15 +33,20 @@
     return lax.all_to_all(value, "col", 0, 0, axis_index_groups=[group], tiled=True)
 
 
+def turned(count):
+    return 2 * (count // 3) + 2
+
+
 def exchange_asks(asks):
     count = asks.shape[0]
-    group = [(row + count // 2) % count for row in range(count)]
-    asks = jnp.roll(asks, -(count // 2), axis=0)
+    group = [(row + turned(count)) % count for row in range(count)]
+    asks = jnp.roll(asks, -turned(count), axis=0)
     return lax.all_to_all(asks, "col", 0, 0, axis_index_groups=[group], tiled=True)
 
 
 def asks_row(place, count):
-    return lax.rem(count + 1 - place, count)
+    row = (first_of(count) - turned(count)) % count - place
+    return jnp.where(row < 0, row + count, row)
 
 
 def pick_kernel(lists, asks, *refs):

time: 256 us -> 255 us (level)
  no operation moved by 1% of the time
where the time goes in v4:
time: 255 us; the launch traced here: 254 us
  waiting for transfers between devices  168 us (66%)
  starting transfers between devices  44.4 us (17%)
  blocking collectives  21.7 us (9%)
  Pallas kernels  17.2 us (7%)
    all_to_all x3, waiting for transfers between devices, exchange(): lax.all_to_all(value, 'col', 0, 0, axis_index_groups=[group], tiled=True)  155 us
    all_to_all x3, starting transfers between devices, exchange(): lax.all_to_all(value, 'col', 0, 0, axis_index_groups=[group], tiled=True)  38.2 us
    all_to_all x1, blocking collectives, exchange_asks(): lax.all_to_all(asks, 'col', 0, 0, axis_index_groups=[group], tiled=True)  21.7 us
    ppermute x2, waiting for transfers between devices, from_partner(): return lax.ppermute(value, 'leaf', pairs)  13 us
    pallas_call x2, Pallas kernels, paired_call(): pl.pallas_call(body, out_shape=jax.ShapeDtypeStruct(local[0].shape, BF16)...  9.93 us
    pallas_call x3, Pallas kernels, pick(): pl.pallas_call(functools.partial(pick_kernel, lists), out_shape=jax.Shape...  7.23 us
    ppermute x2, starting transfers between devices, from_partner(): return lax.ppermute(value, 'leaf', pairs)  6.23 us
  transfers between devices with their start and end apart: 5, of which 4 were waited for; matrix products, arithmetic and copies ran while one was open for 0% of the time, Pallas kernels for 4%

profile of v4, /device:TPU:1, one launch (start us, length us, event | category | flops | bytes accessed | tf_op | source)
XLA Modules:
  0.0 254.5 jit_solution(43429634841672234)
XLA Ops:
  0.0 4.0 %collective-permute-start = (bf16[16,128,128]{2,1,0:T(8,128)(2,1)}, bf16[16,128,128]{2,1,0:T(8,128)(2,1)S(1)}, u32[]{:S(2)}, u32[]{:S(2)}) collective-permute-start(bf16[16,128,128]{2,1,0:T(8,128)(2,1)} %bitcast.11), channel_id=1, source_target_pairs={{0,32},{32,0},{64,96},{96,64},{128,160},{160,128},{192,224},{224,1... | collective-permute-start | bytes 1572872 | tf_op jit(solution)/shard_map/ppermute | solution.py:19
  4.0 0.7 pad_add_fusion
  4.7 0.1 slice.8
  4.8 0.1 add_bitcast_fusion
  4.9 0.1 copy.14
  5.0 21.7 %all_to_all.26 = s32[32,1,4]{2,1,0:T(1,128)} all-to-all(s32[32,1,4]{2,1,0:T(1,128)S(1)} %copy.14), channel_id=1, replica_groups={{22,23,24,25,26,27,28,29,30,31,0,1,2,3,4,5,6,7,8,9,10,11,12,13,14,15,16..., dimensions={0} | all-to-all | bytes 1024 | tf_op jit(solution)/shard_map/all_to_all | solution.py:44
  26.6 0.0 collective-permute-done.refs_2_.refs_1_
  26.7 0.8 copy-done.3
  27.4 2.7 %pick_s_zt.1 = bf16[32,2,128,128]{3,2,1,0:T(8,128)(2,1)} custom-call(s32[32,4]{1,0:T(8,128)} %bitcast.17, bf16[16,128,128]{2,1,0:T(8,128)(2,1)} %bitcast.16, bf16[16,128,128]{2,1,0:T(8,128)(2,1)} %bitcast.12, bf16[16,128,128]{2,1,0:T(8,128)(2,1)} %copy-done.3), custom_call_target="tpu_custom_call" | custom-call | bytes 6291456 | tf_op jit(solution)/shard_map/pick_s_zt/pallas_call | solution.py:92
  30.2 12.2 %all-to-all-start.1 = ((bf16[32,2,128,128]{3,2,1,0:T(8,128)(2,1)}), bf16[32,2,128,128]{3,2,1,0:T(8,128)(2,1)S(1)}, u32[]{:S(2)}, u32[]{:S(2)}) async-start(bf16[32,2,128,128]{3,2,1,0:T(8,128)(2,1)} %pick_s_zt.1), calls=%async_computation.1 | async-start | bytes 4194304 | tf_op jit(solution)/shard_map/all_to_all | solution.py:33
  42.4 0.0 copy-start.5
  42.4 0.0 copy-start.6
  42.4 0.0 copy-start
  42.5 2.3 pick_z.1
  44.7 87.9 %all-to-all-done.1.fetched = bf16[32,2,128,128]{3,2,1,0:T(8,128)(2,1)S(1)} async-done(((bf16[32,2,128,128]{3,2,1,0:T(8,128)(2,1)}), bf16[32,2,128,128]{3,2,1,0:T(8,128)(2,1)S(1)}, u32[]{:S(2)}, u32[]{:S(2)}) %all-to-all-start.1) | async-done | bytes 2097184 | tf_op jit(solution)/shard_map/all_to_all | solution.py:33
  132.6 13.3 %all-to-all-start.3 = ((bf16[32,1,128,128]{3,2,1,0:T(8,128)(2,1)}), bf16[32,1,128,128]{3,2,1,0:T(8,128)(2,1)}, u32[]{:S(2)}, u32[]{:S(2)}) async-start(bf16[32,1,128,128]{3,2,1,0:T(8,128)(2,1)} %pick_z.1), calls=%async_computation.3 | async-start | bytes 2097152 | tf_op jit(solution)/shard_map/all_to_all | solution.py:33
  145.9 0.0 copy-done.5
  145.9 0.0 copy-done.6
  146.0 5.7 %make_d.1.d = bf16[2,8,128,128]{3,2,1,0:T(8,128)(2,1)S(1)} custom-call(s32[2,8,8]{2,1,0:T(8,128)S(1)} %get-tuple-element.9.y_pairs, s32[2,8,8]{2,1,0:T(8,128)S(1)} %get-tuple-element.10.d_pairs, bf16[32,2,128,128]{3,2,1,0:T(8,128)(2,1)S(1)} %all-to-all-done.1.fetched, bf16[2,8,128,128]{3,2,1,0:T(8,128)(2,1)S(1)} %copy-done), custom_call_target="tpu_custom_call" | custom-call | flops 1073741824 | bytes 16777216 | tf_op jit(solution)/shard_map/make_d/pallas_call | solution.py:170
  151.7 0.0 copy-start.1
  151.7 0.0 copy-start.7
  151.7 0.0 copy-start.8
  151.7 2.2 collective-permute-start.1
  153.9 13.0 %collective-permute-done.1.refs_1_ = bf16[16,128,128]{2,1,0:T(8,128)(2,1)S(1)} collective-permute-done((bf16[16,128,128]{2,1,0:T(8,128)(2,1)S(1)}, bf16[16,128,128]{2,1,0:T(8,128)(2,1)S(1)}, u32[]{:S(2)}, u32[]{:S(2)}) %collective-permute-start.1) | collective-permute-done | bytes 524320 | tf_op jit(solution)/shard_map/ppermute | solution.py:19
  166.9 0.8 copy-done.4
  167.7 2.2 pick_d.1
  170.0 0.0 copy-start.2
  170.0 21.8 %all-to-all-done.3.z_fetched = bf16[32,1,128,128]{3,2,1,0:T(8,128)(2,1)} async-done(((bf16[32,1,128,128]{3,2,1,0:T(8,128)(2,1)}), bf16[32,1,128,128]{3,2,1,0:T(8,128)(2,1)}, u32[]{:S(2)}, u32[]{:S(2)}) %all-to-all-start.3) | async-done | bytes 1048608 | tf_op jit(solution)/shard_map/all_to_all | solution.py:33
  191.8 12.6 %all-to-all-start.2 = ((bf16[32,1,128,128]{3,2,1,0:T(8,128)(2,1)}), bf16[32,1,128,128]{3,2,1,0:T(8,128)(2,1)S(1)}, u32[]{:S(2)}, u32[]{:S(2)}) async-start(bf16[32,1,128,128]{3,2,1,0:T(8,128)(2,1)} %pick_d.1), calls=%async_computation.2 | async-start | bytes 2097152 | tf_op jit(solution)/shard_map/all_to_all | solution.py:33
  204.5 45.8 %all-to-all-done.2.d_fetched = bf16[32,1,128,128]{3,2,1,0:T(8,128)(2,1)S(1)} async-done(((bf16[32,1,128,128]{3,2,1,0:T(8,128)(2,1)}), bf16[32,1,128,128]{3,2,1,0:T(8,128)(2,1)S(1)}, u32[]{:S(2)}, u32[]{:S(2)}) %all-to-all-start.2) | async-done | bytes 1048608 | tf_op jit(solution)/shard_map/all_to_all | solution.py:33
  250.3 0.0 copy-done.2
  250.3 4.2 %refine.1 = bf16[2,8,128,128]{3,2,1,0:T(8,128)(2,1)} custom-call(s32[2,8,8]{2,1,0:T(8,128)S(1)} %get-tuple-element.11.e_pairs, s32[2,8,8]{2,1,0:T(8,128)S(1)} %get-tuple-element.12.z_pairs, bf16[32,1,128,128]{3,2,1,0:T(8,128)(2,1)S(1)} %all-to-all-done.2.d_fetched, bf16[32,1,128,128]{3,2,1,0:T(8,128)(2,1)} %all-to-all-done.3.z_fetched, ...), custom_call_target="tpu_custom_call" | custom-call | flops 1073741824 | bytes 16777216 | tf_op jit(solution)/shard_map/refine/pallas_call | solution.py:170
  (8 shorter events, 0.0 us)
Async XLA Ops:
  0.0 26.6 %collective-permute-start = (bf16[16,128,128]{2,1,0:T(8,128)(2,1)}, bf16[16,128,128]{2,1,0:T(8,128)(2,1)S(1)}, u32[]{:S(2)}, u32[]{:S(2)}) collective-permute-start(bf16[16,128,128]{2,1,0:T(8,128)(2,1)} %bitcast.11), channel_id=1, source_target_pairs={{0,32},{32,0},{64,96},{96,64},{128,160},{160,128},{192,224},{224,1... | collective-permute-start | bytes 1572872 | tf_op jit(solution)/shard_map/ppermute | solution.py:19
  26.7 0.8 copy-start.3
  30.2 102.4 %all-to-all-start.1 = ((bf16[32,2,128,128]{3,2,1,0:T(8,128)(2,1)}), bf16[32,2,128,128]{3,2,1,0:T(8,128)(2,1)S(1)}, u32[]{:S(2)}, u32[]{:S(2)}) async-start(bf16[32,2,128,128]{3,2,1,0:T(8,128)(2,1)} %pick_s_zt.1), calls=%async_computation.1 | async-start | bytes 4194304 | tf_op jit(solution)/shard_map/all_to_all | solution.py:33
  42.4 103.5 %copy-start.5 = (s32[2,8,8]{2,1,0:T(8,128)S(1)}, s32[2,8,8]{2,1,0:T(8,128)}, u32[]{:S(2)}) copy-start(s32[2,8,8]{2,1,0:T(8,128)} %param.13) | copy-start | bytes 1540
  42.4 103.5 %copy-start.6 = (s32[2,8,8]{2,1,0:T(8,128)S(1)}, s32[2,8,8]{2,1,0:T(8,128)}, u32[]{:S(2)}) copy-start(s32[2,8,8]{2,1,0:T(8,128)} %param.15) | copy-start | bytes 1540
  42.4 103.5 %copy-start = (bf16[2,8,128,128]{3,2,1,0:T(8,128)(2,1)S(1)}, bf16[2,8,128,128]{3,2,1,0:T(8,128)(2,1)}, u32[]{:S(2)}) copy-start(bf16[2,8,128,128]{3,2,1,0:T(8,128)(2,1)} %z.3) | copy-start | bytes 1572868
  132.6 59.2 %all-to-all-start.3 = ((bf16[32,1,128,128]{3,2,1,0:T(8,128)(2,1)}), bf16[32,1,128,128]{3,2,1,0:T(8,128)(2,1)}, u32[]{:S(2)}, u32[]{:S(2)}) async-start(bf16[32,1,128,128]{3,2,1,0:T(8,128)(2,1)} %pick_z.1), calls=%async_computation.3 | async-start | bytes 2097152 | tf_op jit(solution)/shard_map/all_to_all | solution.py:33
  151.7 15.2 %copy-start.1 = (bf16[2,8,128,128]{3,2,1,0:T(8,128)(2,1)}, bf16[2,8,128,128]{3,2,1,0:T(8,128)(2,1)S(1)}, u32[]{:S(2)}) copy-start(bf16[2,8,128,128]{3,2,1,0:T(8,128)(2,1)S(1)} %make_d.1.d) | copy-start | bytes 1572868
  151.7 52.7 %copy-start.7 = (s32[2,8,8]{2,1,0:T(8,128)S(1)}, s32[2,8,8]{2,1,0:T(8,128)}, u32[]{:S(2)}) copy-start(s32[2,8,8]{2,1,0:T(8,128)} %param.17) | copy-start | bytes 1540
  151.7 52.7 %copy-start.8 = (s32[2,8,8]{2,1,0:T(8,128)S(1)}, s32[2,8,8]{2,1,0:T(8,128)}, u32[]{:S(2)}) copy-start(s32[2,8,8]{2,1,0:T(8,128)} %param.19) | copy-start | bytes 1540
  151.7 15.2 %collective-permute-start.1 = (bf16[16,128,128]{2,1,0:T(8,128)(2,1)S(1)}, bf16[16,128,128]{2,1,0:T(8,128)(2,1)S(1)}, u32[]{:S(2)}, u32[]{:S(2)}) collective-permute-start(bf16[16,128,128]{2,1,0:T(8,128)(2,1)S(1)} %bitcast.14), channel_id=1, source_target_pairs={{0,32},{32,0},{64,96},{96,64},{128,160},{160,128},{192,224},{224,1... | collective-permute-start | bytes 1572872 | tf_op jit(solution)/shard_map/ppermute | solution.py:19
  166.9 0.8 copy-start.4
  170.0 80.3 %copy-start.2 = (bf16[2,8,128,128]{3,2,1,0:T(8,128)(2,1)S(1)}, bf16[2,8,128,128]{3,2,1,0:T(8,128)(2,1)}, u32[]{:S(2)}) copy-start(bf16[2,8,128,128]{3,2,1,0:T(8,128)(2,1)} %copy-done.1) | copy-start | bytes 1572868
  191.8 58.5 %all-to-all-start.2 = ((bf16[32,1,128,128]{3,2,1,0:T(8,128)(2,1)}), bf16[32,1,128,128]{3,2,1,0:T(8,128)(2,1)S(1)}, u32[]{:S(2)}, u32[]{:S(2)}) async-start(bf16[32,1,128,128]{3,2,1,0:T(8,128)(2,1)} %pick_d.1), calls=%async_computation.2 | async-start | bytes 2097152 | tf_op jit(solution)/shard_map/all_to_all | solution.py:33

commit v5 on v4

--- a/solution.py
+++ b/solution.py
@@ -20,7 +20,7 @@
 
 
 def first_of(count):
-    return count // 2 + 1
+    return count // 2 + 5
 
 
 def standing(peer, count):

time: 255 us -> 254 us (level)
  starting transfers between devices: 44.4 us -> 39.3 us
  waiting for transfers between devices: 168 us -> 173 us
    all_to_all x3, starting transfers between devices: 38.2 us -> 33 us  [exchange(): lax.all_to_all(value, 'col', 0, 0, axis_index_groups=[group], tiled=True)]
    all_to_all x3, waiting for transfers between devices: 155 us -> 160 us  [exchange(): lax.all_to_all(value, 'col', 0, 0, axis_index_groups=[group], tiled=True)]
where the time goes in v5:
time: 254 us
  waiting for transfers between devices  173 us (68%)
  starting transfers between devices  39.3 us (15%)
  blocking collectives  21.7 us (9%)
  Pallas kernels  17.2 us (7%)
    all_to_all x3, waiting for transfers between devices, exchange(): lax.all_to_all(value, 'col', 0, 0, axis_index_groups=[group], tiled=True)  160 us
    all_to_all x3, starting transfers between devices, exchange(): lax.all_to_all(value, 'col', 0, 0, axis_index_groups=[group], tiled=True)  33 us
    all_to_all x1, blocking collectives, exchange_asks(): lax.all_to_all(asks, 'col', 0, 0, axis_index_groups=[group], tiled=True)  21.7 us
    ppermute x2, waiting for transfers between devices, from_partner(): return lax.ppermute(value, 'leaf', pairs)  13 us
    pallas_call x2, Pallas kernels, paired_call(): pl.pallas_call(body, out_shape=jax.ShapeDtypeStruct(local[0].shape, BF16)...  9.93 us
    pallas_call x3, Pallas kernels, pick(): pl.pallas_call(functools.partial(pick_kernel, lists), out_shape=jax.Shape...  7.23 us
    ppermute x2, starting transfers between devices, from_partner(): return lax.ppermute(value, 'leaf', pairs)  6.23 us
  transfers between devices with their start and end apart: 5, of which 4 were waited for; matrix products, arithmetic and copies ran while one was open for 0% of the time, Pallas kernels for 4%

profile of v5, /device:TPU:1, one launch (start us, length us, event | category | flops | bytes accessed | tf_op | source)
XLA Modules:
  0.0 253.9 jit_solution(14690769657612272038)
XLA Ops:
  0.0 4.0 %collective-permute-start = (bf16[16,128,128]{2,1,0:T(8,128)(2,1)}, bf16[16,128,128]{2,1,0:T(8,128)(2,1)S(1)}, u32[]{:S(2)}, u32[]{:S(2)}) collective-permute-start(bf16[16,128,128]{2,1,0:T(8,128)(2,1)} %bitcast.11), channel_id=1, source_target_pairs={{0,32},{32,0},{64,96},{96,64},{128,160},{160,128},{192,224},{224,1... | collective-permute-start | bytes 1572872 | tf_op jit(solution)/shard_map/ppermute | solution.py:19
  4.0 0.7 pad_add_fusion
  4.7 0.1 slice.8
  4.8 0.1 add_bitcast_fusion
  4.9 0.1 copy.14
  5.0 21.7 %all_to_all.26 = s32[32,1,4]{2,1,0:T(1,128)} all-to-all(s32[32,1,4]{2,1,0:T(1,128)S(1)} %copy.14), channel_id=1, replica_groups={{22,23,24,25,26,27,28,29,30,31,0,1,2,3,4,5,6,7,8,9,10,11,12,13,14,15,16..., dimensions={0} | all-to-all | bytes 1024 | tf_op jit(solution)/shard_map/all_to_all | solution.py:44
  26.6 0.0 collective-permute-done.refs_2_.refs_1_
  26.7 0.8 copy-done.3
  27.4 2.7 %pick_s_zt.1 = bf16[32,2,128,128]{3,2,1,0:T(8,128)(2,1)} custom-call(s32[32,4]{1,0:T(8,128)} %bitcast.17, bf16[16,128,128]{2,1,0:T(8,128)(2,1)} %bitcast.16, bf16[16,128,128]{2,1,0:T(8,128)(2,1)} %bitcast.12, bf16[16,128,128]{2,1,0:T(8,128)(2,1)} %copy-done.3), custom_call_target="tpu_custom_call" | custom-call | bytes 6291456 | tf_op jit(solution)/shard_map/pick_s_zt/pallas_call | solution.py:92
  30.2 10.7 %all-to-all-start.1 = ((bf16[32,2,128,128]{3,2,1,0:T(8,128)(2,1)}), bf16[32,2,128,128]{3,2,1,0:T(8,128)(2,1)S(1)}, u32[]{:S(2)}, u32[]{:S(2)}) async-start(bf16[32,2,128,128]{3,2,1,0:T(8,128)(2,1)} %pick_s_zt.1), calls=%async_computation.1 | async-start | bytes 4194304 | tf_op jit(solution)/shard_map/all_to_all | solution.py:33
  40.9 0.0 copy-start.5
  40.9 0.0 copy-start.6
  40.9 0.0 copy-start
  40.9 2.3 pick_z.1
  43.2 90.6 %all-to-all-done.1.fetched = bf16[32,2,128,128]{3,2,1,0:T(8,128)(2,1)S(1)} async-done(((bf16[32,2,128,128]{3,2,1,0:T(8,128)(2,1)}), bf16[32,2,128,128]{3,2,1,0:T(8,128)(2,1)S(1)}, u32[]{:S(2)}, u32[]{:S(2)}) %all-to-all-start.1) | async-done | bytes 2097184 | tf_op jit(solution)/shard_map/all_to_all | solution.py:33
  133.9 10.5 %all-to-all-start.3 = ((bf16[32,1,128,128]{3,2,1,0:T(8,128)(2,1)}), bf16[32,1,128,128]{3,2,1,0:T(8,128)(2,1)}, u32[]{:S(2)}, u32[]{:S(2)}) async-start(bf16[32,1,128,128]{3,2,1,0:T(8,128)(2,1)} %pick_z.1), calls=%async_computation.3 | async-start | bytes 2097152 | tf_op jit(solution)/shard_map/all_to_all | solution.py:33
  144.4 0.0 copy-done.5
  144.4 0.0 copy-done.6
  144.5 0.0 copy-done
  144.5 5.7 %make_d.1.d = bf16[2,8,128,128]{3,2,1,0:T(8,128)(2,1)S(1)} custom-call(s32[2,8,8]{2,1,0:T(8,128)S(1)} %get-tuple-element.9.y_pairs, s32[2,8,8]{2,1,0:T(8,128)S(1)} %get-tuple-element.10.d_pairs, bf16[32,2,128,128]{3,2,1,0:T(8,128)(2,1)S(1)} %all-to-all-done.1.fetched, bf16[2,8,128,128]{3,2,1,0:T(8,128)(2,1)S(1)} %copy-done), custom_call_target="tpu_custom_call" | custom-call | flops 1073741824 | bytes 16777216 | tf_op jit(solution)/shard_map/make_d/pallas_call | solution.py:170
  150.2 0.0 copy-start.1
  150.2 0.0 copy-start.7
  150.2 0.0 copy-start.8
  150.2 2.2 collective-permute-start.1
  152.4 13.0 %collective-permute-done.1.refs_1_ = bf16[16,128,128]{2,1,0:T(8,128)(2,1)S(1)} collective-permute-done((bf16[16,128,128]{2,1,0:T(8,128)(2,1)S(1)}, bf16[16,128,128]{2,1,0:T(8,128)(2,1)S(1)}, u32[]{:S(2)}, u32[]{:S(2)}) %collective-permute-start.1) | collective-permute-done | bytes 524320 | tf_op jit(solution)/shard_map/ppermute | solution.py:19
  165.4 0.8 copy-done.4
  166.2 2.2 pick_d.1
  168.5 0.0 copy-start.2
  168.5 22.7 %all-to-all-done.3.z_fetched = bf16[32,1,128,128]{3,2,1,0:T(8,128)(2,1)} async-done(((bf16[32,1,128,128]{3,2,1,0:T(8,128)(2,1)}), bf16[32,1,128,128]{3,2,1,0:T(8,128)(2,1)}, u32[]{:S(2)}, u32[]{:S(2)}) %all-to-all-start.3) | async-done | bytes 1048608 | tf_op jit(solution)/shard_map/all_to_all | solution.py:33
  191.2 11.8 %all-to-all-start.2 = ((bf16[32,1,128,128]{3,2,1,0:T(8,128)(2,1)}), bf16[32,1,128,128]{3,2,1,0:T(8,128)(2,1)S(1)}, u32[]{:S(2)}, u32[]{:S(2)}) async-start(bf16[32,1,128,128]{3,2,1,0:T(8,128)(2,1)} %pick_d.1), calls=%async_computation.2 | async-start | bytes 2097152 | tf_op jit(solution)/shard_map/all_to_all | solution.py:33
  203.0 46.7 %all-to-all-done.2.d_fetched = bf16[32,1,128,128]{3,2,1,0:T(8,128)(2,1)S(1)} async-done(((bf16[32,1,128,128]{3,2,1,0:T(8,128)(2,1)}), bf16[32,1,128,128]{3,2,1,0:T(8,128)(2,1)S(1)}, u32[]{:S(2)}, u32[]{:S(2)}) %all-to-all-start.2) | async-done | bytes 1048608 | tf_op jit(solution)/shard_map/all_to_all | solution.py:33
  249.7 4.2 %refine.1 = bf16[2,8,128,128]{3,2,1,0:T(8,128)(2,1)} custom-call(s32[2,8,8]{2,1,0:T(8,128)S(1)} %get-tuple-element.11.e_pairs, s32[2,8,8]{2,1,0:T(8,128)S(1)} %get-tuple-element.12.z_pairs, bf16[32,1,128,128]{3,2,1,0:T(8,128)(2,1)S(1)} %all-to-all-done.2.d_fetched, bf16[32,1,128,128]{3,2,1,0:T(8,128)(2,1)} %all-to-all-done.3.z_fetched, ...), custom_call_target="tpu_custom_call" | custom-call | flops 1073741824 | bytes 16777216 | tf_op jit(solution)/shard_map/refine/pallas_call | solution.py:170
  (8 shorter events, 0.0 us)
Async XLA Ops:
  0.0 26.6 %collective-permute-start = (bf16[16,128,128]{2,1,0:T(8,128)(2,1)}, bf16[16,128,128]{2,1,0:T(8,128)(2,1)S(1)}, u32[]{:S(2)}, u32[]{:S(2)}) collective-permute-start(bf16[16,128,128]{2,1,0:T(8,128)(2,1)} %bitcast.11), channel_id=1, source_target_pairs={{0,32},{32,0},{64,96},{96,64},{128,160},{160,128},{192,224},{224,1... | collective-permute-start | bytes 1572872 | tf_op jit(solution)/shard_map/ppermute | solution.py:19
  26.7 0.8 copy-start.3
  30.2 103.7 %all-to-all-start.1 = ((bf16[32,2,128,128]{3,2,1,0:T(8,128)(2,1)}), bf16[32,2,128,128]{3,2,1,0:T(8,128)(2,1)S(1)}, u32[]{:S(2)}, u32[]{:S(2)}) async-start(bf16[32,2,128,128]{3,2,1,0:T(8,128)(2,1)} %pick_s_zt.1), calls=%async_computation.1 | async-start | bytes 4194304 | tf_op jit(solution)/shard_map/all_to_all | solution.py:33
  40.9 103.5 %copy-start.5 = (s32[2,8,8]{2,1,0:T(8,128)S(1)}, s32[2,8,8]{2,1,0:T(8,128)}, u32[]{:S(2)}) copy-start(s32[2,8,8]{2,1,0:T(8,128)} %param.13) | copy-start | bytes 1540
  40.9 103.5 %copy-start.6 = (s32[2,8,8]{2,1,0:T(8,128)S(1)}, s32[2,8,8]{2,1,0:T(8,128)}, u32[]{:S(2)}) copy-start(s32[2,8,8]{2,1,0:T(8,128)} %param.15) | copy-start | bytes 1540
  40.9 103.5 %copy-start = (bf16[2,8,128,128]{3,2,1,0:T(8,128)(2,1)S(1)}, bf16[2,8,128,128]{3,2,1,0:T(8,128)(2,1)}, u32[]{:S(2)}) copy-start(bf16[2,8,128,128]{3,2,1,0:T(8,128)(2,1)} %z.3) | copy-start | bytes 1572868
  133.9 57.3 %all-to-all-start.3 = ((bf16[32,1,128,128]{3,2,1,0:T(8,128)(2,1)}), bf16[32,1,128,128]{3,2,1,0:T(8,128)(2,1)}, u32[]{:S(2)}, u32[]{:S(2)}) async-start(bf16[32,1,128,128]{3,2,1,0:T(8,128)(2,1)} %pick_z.1), calls=%async_computation.3 | async-start | bytes 2097152 | tf_op jit(solution)/shard_map/all_to_all | solution.py:33
  150.2 15.2 %copy-start.1 = (bf16[2,8,128,128]{3,2,1,0:T(8,128)(2,1)}, bf16[2,8,128,128]{3,2,1,0:T(8,128)(2,1)S(1)}, u32[]{:S(2)}) copy-start(bf16[2,8,128,128]{3,2,1,0:T(8,128)(2,1)S(1)} %make_d.1.d) | copy-start | bytes 1572868
  150.2 52.8 %copy-start.7 = (s32[2,8,8]{2,1,0:T(8,128)S(1)}, s32[2,8,8]{2,1,0:T(8,128)}, u32[]{:S(2)}) copy-start(s32[2,8,8]{2,1,0:T(8,128)} %param.17) | copy-start | bytes 1540
  150.2 52.8 %copy-start.8 = (s32[2,8,8]{2,1,0:T(8,128)S(1)}, s32[2,8,8]{2,1,0:T(8,128)}, u32[]{:S(2)}) copy-start(s32[2,8,8]{2,1,0:T(8,128)} %param.19) | copy-start | bytes 1540
  150.2 15.2 %collective-permute-start.1 = (bf16[16,128,128]{2,1,0:T(8,128)(2,1)S(1)}, bf16[16,128,128]{2,1,0:T(8,128)(2,1)S(1)}, u32[]{:S(2)}, u32[]{:S(2)}) collective-permute-start(bf16[16,128,128]{2,1,0:T(8,128)(2,1)S(1)} %bitcast.14), channel_id=1, source_target_pairs={{0,32},{32,0},{64,96},{96,64},{128,160},{160,128},{192,224},{224,1... | collective-permute-start | bytes 1572872 | tf_op jit(solution)/shard_map/ppermute | solution.py:19
  165.4 0.8 copy-start.4
  168.5 81.2 %copy-start.2 = (bf16[2,8,128,128]{3,2,1,0:T(8,128)(2,1)S(1)}, bf16[2,8,128,128]{3,2,1,0:T(8,128)(2,1)}, u32[]{:S(2)}) copy-start(bf16[2,8,128,128]{3,2,1,0:T(8,128)(2,1)} %copy-done.1) | copy-start | bytes 1572868
  191.2 58.5 %all-to-all-start.2 = ((bf16[32,1,128,128]{3,2,1,0:T(8,128)(2,1)}), bf16[32,1,128,128]{3,2,1,0:T(8,128)(2,1)S(1)}, u32[]{:S(2)}, u32[]{:S(2)}) async-start(bf16[32,1,128,128]{3,2,1,0:T(8,128)(2,1)} %pick_d.1), calls=%async_computation.2 | async-start | bytes 2097152 | tf_op jit(solution)/shard_map/all_to_all | solution.py:33

commit v6 on v5

--- a/solution.py
+++ b/solution.py
@@ -56,25 +56,28 @@
     readers = out.shape[0]
     ask_copy = pltpu.make_async_copy(asks, asked, in_sems.at[in_sems.shape[0] - 1])
     ask_copy.start()
-    copies, sizes = [], []
+    loads, sizes = [], []
     for store, (_, begin, end) in zip(stores, lists):
-        first = 0
+        first, mine = 0, []
         for h in range(begin, end):
             count = held[h].shape[0]
-            copies.append(pltpu.make_async_copy(held[h], store.at[pl.ds(first, count)], in_sems.at[len(copies)]))
+            load_sem = in_sems.at[sum(map(len, loads)) + len(mine)]
+            mine.append(pltpu.make_async_copy(held[h], store.at[pl.ds(first, count)], load_sem))
             first += count
+        loads.append(mine)
         sizes.append(first)
-    for copy in copies:
-        copy.start()
+    for mine in loads:
+        for load in mine:
+            load.start()
     for store, size in zip(stores, sizes):
         store[size] = jnp.zeros(store.shape[1:], BF16)
     ask_copy.wait()
-    for copy in copies:
-        copy.wait()
-
-    @pl.loop(0, readers)
-    def _(reader):
-        for place, (store, size, (row, _, _)) in enumerate(zip(stores, sizes, lists)):
+    for place, (store, size, mine, (row, _, _)) in enumerate(zip(stores, sizes, loads, lists)):
+        for load in mine:
+            load.wait()
+
+        @pl.loop(0, readers)
+        def _(reader):
             slot = asked[asks_row(reader, readers), row]
             at = jnp.where(slot < 0, size, slot)
             pltpu.make_async_copy(store.at[at], out.at[reader, place], sem).start()

time: 254 us -> 254 us (level)
  no operation moved by 1% of the time
where the time goes in v6:
time: 254 us
  waiting for transfers between devices  173 us (68%)
  starting transfers between devices  39.3 us (15%)
  blocking collectives  21.7 us (9%)
  Pallas kernels  16.9 us (7%)
    all_to_all x3, waiting for transfers between devices, exchange(): lax.all_to_all(value, 'col', 0, 0, axis_index_groups=[group], tiled=True)  160 us
    all_to_all x3, starting transfers between devices, exchange(): lax.all_to_all(value, 'col', 0, 0, axis_index_groups=[group], tiled=True)  33 us
    all_to_all x1, blocking collectives, exchange_asks(): lax.all_to_all(asks, 'col', 0, 0, axis_index_groups=[group], tiled=True)  21.7 us
    ppermute x2, waiting for transfers between devices, from_partner(): return lax.ppermute(value, 'leaf', pairs)  13 us
    pallas_call x2, Pallas kernels, paired_call(): pl.pallas_call(body, out_shape=jax.ShapeDtypeStruct(local[0].shape, BF16)...  9.93 us
    pallas_call x3, Pallas kernels, pick(): pl.pallas_call(functools.partial(pick_kernel, lists), out_shape=jax.Shape...  6.93 us
    ppermute x2, starting transfers between devices, from_partner(): return lax.ppermute(value, 'leaf', pairs)  6.23 us
  transfers between devices with their start and end apart: 5, of which 4 were waited for; matrix products, arithmetic and copies ran while one was open for 0% of the time, Pallas kernels for 4%

profile of v6, /device:TPU:1, one launch (start us, length us, event | category | flops | bytes accessed | tf_op | source)
XLA Modules:
  0.0 253.6 jit_solution(14800167535689777388)
XLA Ops:
  0.0 4.0 %collective-permute-start = (bf16[16,128,128]{2,1,0:T(8,128)(2,1)}, bf16[16,128,128]{2,1,0:T(8,128)(2,1)S(1)}, u32[]{:S(2)}, u32[]{:S(2)}) collective-permute-start(bf16[16,128,128]{2,1,0:T(8,128)(2,1)} %bitcast.11), channel_id=1, source_target_pairs={{0,32},{32,0},{64,96},{96,64},{128,160},{160,128},{192,224},{224,1... | collective-permute-start | bytes 1572872 | tf_op jit(solution)/shard_map/ppermute | solution.py:19
  4.0 0.7 pad_add_fusion
  4.7 0.1 slice.8
  4.8 0.1 add_bitcast_fusion
  4.9 0.1 copy.14
  5.0 21.7 %all_to_all.26 = s32[32,1,4]{2,1,0:T(1,128)} all-to-all(s32[32,1,4]{2,1,0:T(1,128)S(1)} %copy.14), channel_id=1, replica_groups={{22,23,24,25,26,27,28,29,30,31,0,1,2,3,4,5,6,7,8,9,10,11,12,13,14,15,16..., dimensions={0} | all-to-all | bytes 1024 | tf_op jit(solution)/shard_map/all_to_all | solution.py:44
  26.6 0.0 collective-permute-done.refs_2_.refs_1_
  26.7 0.8 copy-done.3
  27.4 2.4 pick_s_zt.1
  29.9 10.7 %all-to-all-start.1 = ((bf16[32,2,128,128]{3,2,1,0:T(8,128)(2,1)}), bf16[32,2,128,128]{3,2,1,0:T(8,128)(2,1)S(1)}, u32[]{:S(2)}, u32[]{:S(2)}) async-start(bf16[32,2,128,128]{3,2,1,0:T(8,128)(2,1)} %pick_s_zt.1), calls=%async_computation.1 | async-start | bytes 4194304 | tf_op jit(solution)/shard_map/all_to_all | solution.py:33
  40.6 0.0 copy-start.5
  40.6 0.0 copy-start.6
  40.6 0.0 copy-start
  40.6 2.3 pick_z.1
  42.9 90.6 %all-to-all-done.1.fetched = bf16[32,2,128,128]{3,2,1,0:T(8,128)(2,1)S(1)} async-done(((bf16[32,2,128,128]{3,2,1,0:T(8,128)(2,1)}), bf16[32,2,128,128]{3,2,1,0:T(8,128)(2,1)S(1)}, u32[]{:S(2)}, u32[]{:S(2)}) %all-to-all-start.1) | async-done | bytes 2097184 | tf_op jit(solution)/shard_map/all_to_all | solution.py:33
  133.6 10.5 %all-to-all-start.3 = ((bf16[32,1,128,128]{3,2,1,0:T(8,128)(2,1)}), bf16[32,1,128,128]{3,2,1,0:T(8,128)(2,1)}, u32[]{:S(2)}, u32[]{:S(2)}) async-start(bf16[32,1,128,128]{3,2,1,0:T(8,128)(2,1)} %pick_z.1), calls=%async_computation.3 | async-start | bytes 2097152 | tf_op jit(solution)/shard_map/all_to_all | solution.py:33
  144.1 0.0 copy-done.5
  144.2 5.7 %make_d.1.d = bf16[2,8,128,128]{3,2,1,0:T(8,128)(2,1)S(1)} custom-call(s32[2,8,8]{2,1,0:T(8,128)S(1)} %get-tuple-element.9.y_pairs, s32[2,8,8]{2,1,0:T(8,128)S(1)} %get-tuple-element.10.d_pairs, bf16[32,2,128,128]{3,2,1,0:T(8,128)(2,1)S(1)} %all-to-all-done.1.fetched, bf16[2,8,128,128]{3,2,1,0:T(8,128)(2,1)S(1)} %copy-done), custom_call_target="tpu_custom_call" | custom-call | flops 1073741824 | bytes 16777216 | tf_op jit(solution)/shard_map/make_d/pallas_call | solution.py:173
  149.9 0.0 copy-start.1
  149.9 0.0 copy-start.7
  149.9 0.0 copy-start.8
  149.9 2.2 collective-permute-start.1
  152.1 13.0 %collective-permute-done.1.refs_1_ = bf16[16,128,128]{2,1,0:T(8,128)(2,1)S(1)} collective-permute-done((bf16[16,128,128]{2,1,0:T(8,128)(2,1)S(1)}, bf16[16,128,128]{2,1,0:T(8,128)(2,1)S(1)}, u32[]{:S(2)}, u32[]{:S(2)}) %collective-permute-start.1) | collective-permute-done | bytes 524320 | tf_op jit(solution)/shard_map/ppermute | solution.py:19
  165.1 0.0 copy-done.1
  165.1 0.8 copy-done.4
  165.9 2.2 pick_d.1
  168.2 0.0 copy-start.2
  168.2 22.7 %all-to-all-done.3.z_fetched = bf16[32,1,128,128]{3,2,1,0:T(8,128)(2,1)} async-done(((bf16[32,1,128,128]{3,2,1,0:T(8,128)(2,1)}), bf16[32,1,128,128]{3,2,1,0:T(8,128)(2,1)}, u32[]{:S(2)}, u32[]{:S(2)}) %all-to-all-start.3) | async-done | bytes 1048608 | tf_op jit(solution)/shard_map/all_to_all | solution.py:33
  190.9 11.8 %all-to-all-start.2 = ((bf16[32,1,128,128]{3,2,1,0:T(8,128)(2,1)}), bf16[32,1,128,128]{3,2,1,0:T(8,128)(2,1)S(1)}, u32[]{:S(2)}, u32[]{:S(2)}) async-start(bf16[32,1,128,128]{3,2,1,0:T(8,128)(2,1)} %pick_d.1), calls=%async_computation.2 | async-start | bytes 2097152 | tf_op jit(solution)/shard_map/all_to_all | solution.py:33
  202.7 46.7 %all-to-all-done.2.d_fetched = bf16[32,1,128,128]{3,2,1,0:T(8,128)(2,1)S(1)} async-done(((bf16[32,1,128,128]{3,2,1,0:T(8,128)(2,1)}), bf16[32,1,128,128]{3,2,1,0:T(8,128)(2,1)S(1)}, u32[]{:S(2)}, u32[]{:S(2)}) %all-to-all-start.2) | async-done | bytes 1048608 | tf_op jit(solution)/shard_map/all_to_all | solution.py:33
  249.4 0.0 copy-done.2
  249.4 4.2 %refine.1 = bf16[2,8,128,128]{3,2,1,0:T(8,128)(2,1)} custom-call(s32[2,8,8]{2,1,0:T(8,128)S(1)} %get-tuple-element.11.e_pairs, s32[2,8,8]{2,1,0:T(8,128)S(1)} %get-tuple-element.12.z_pairs, bf16[32,1,128,128]{3,2,1,0:T(8,128)(2,1)S(1)} %all-to-all-done.2.d_fetched, bf16[32,1,128,128]{3,2,1,0:T(8,128)(2,1)} %all-to-all-done.3.z_fetched, ...), custom_call_target="tpu_custom_call" | custom-call | flops 1073741824 | bytes 16777216 | tf_op jit(solution)/shard_map/refine/pallas_call | solution.py:173
  (8 shorter events, 0.0 us)
Async XLA Ops:
  0.0 26.6 %collective-permute-start = (bf16[16,128,128]{2,1,0:T(8,128)(2,1)}, bf16[16,128,128]{2,1,0:T(8,128)(2,1)S(1)}, u32[]{:S(2)}, u32[]{:S(2)}) collective-permute-start(bf16[16,128,128]{2,1,0:T(8,128)(2,1)} %bitcast.11), channel_id=1, source_target_pairs={{0,32},{32,0},{64,96},{96,64},{128,160},{160,128},{192,224},{224,1... | collective-permute-start | bytes 1572872 | tf_op jit(solution)/shard_map/ppermute | solution.py:19
  26.7 0.8 copy-start.3
  29.9 103.7 %all-to-all-start.1 = ((bf16[32,2,128,128]{3,2,1,0:T(8,128)(2,1)}), bf16[32,2,128,128]{3,2,1,0:T(8,128)(2,1)S(1)}, u32[]{:S(2)}, u32[]{:S(2)}) async-start(bf16[32,2,128,128]{3,2,1,0:T(8,128)(2,1)} %pick_s_zt.1), calls=%async_computation.1 | async-start | bytes 4194304 | tf_op jit(solution)/shard_map/all_to_all | solution.py:33
  40.6 103.5 %copy-start.5 = (s32[2,8,8]{2,1,0:T(8,128)S(1)}, s32[2,8,8]{2,1,0:T(8,128)}, u32[]{:S(2)}) copy-start(s32[2,8,8]{2,1,0:T(8,128)} %param.13) | copy-start | bytes 1540
  40.6 103.5 %copy-start.6 = (s32[2,8,8]{2,1,0:T(8,128)S(1)}, s32[2,8,8]{2,1,0:T(8,128)}, u32[]{:S(2)}) copy-start(s32[2,8,8]{2,1,0:T(8,128)} %param.15) | copy-start | bytes 1540
  40.6 103.5 %copy-start = (bf16[2,8,128,128]{3,2,1,0:T(8,128)(2,1)S(1)}, bf16[2,8,128,128]{3,2,1,0:T(8,128)(2,1)}, u32[]{:S(2)}) copy-start(bf16[2,8,128,128]{3,2,1,0:T(8,128)(2,1)} %z.3) | copy-start | bytes 1572868
  133.6 57.3 %all-to-all-start.3 = ((bf16[32,1,128,128]{3,2,1,0:T(8,128)(2,1)}), bf16[32,1,128,128]{3,2,1,0:T(8,128)(2,1)}, u32[]{:S(2)}, u32[]{:S(2)}) async-start(bf16[32,1,128,128]{3,2,1,0:T(8,128)(2,1)} %pick_z.1), calls=%async_computation.3 | async-start | bytes 2097152 | tf_op jit(solution)/shard_map/all_to_all | solution.py:33
  149.9 15.2 %copy-start.1 = (bf16[2,8,128,128]{3,2,1,0:T(8,128)(2,1)}, bf16[2,8,128,128]{3,2,1,0:T(8,128)(2,1)S(1)}, u32[]{:S(2)}) copy-start(bf16[2,8,128,128]{3,2,1,0:T(8,128)(2,1)S(1)} %make_d.1.d) | copy-start | bytes 1572868
  149.9 52.8 %copy-start.7 = (s32[2,8,8]{2,1,0:T(8,128)S(1)}, s32[2,8,8]{2,1,0:T(8,128)}, u32[]{:S(2)}) copy-start(s32[2,8,8]{2,1,0:T(8,128)} %param.17) | copy-start | bytes 1540
  149.9 52.8 %copy-start.8 = (s32[2,8,8]{2,1,0:T(8,128)S(1)}, s32[2,8,8]{2,1,0:T(8,128)}, u32[]{:S(2)}) copy-start(s32[2,8,8]{2,1,0:T(8,128)} %param.19) | copy-start | bytes 1540
  149.9 15.2 %collective-permute-start.1 = (bf16[16,128,128]{2,1,0:T(8,128)(2,1)S(1)}, bf16[16,128,128]{2,1,0:T(8,128)(2,1)S(1)}, u32[]{:S(2)}, u32[]{:S(2)}) collective-permute-start(bf16[16,128,128]{2,1,0:T(8,128)(2,1)S(1)} %bitcast.14), channel_id=1, source_target_pairs={{0,32},{32,0},{64,96},{96,64},{128,160},{160,128},{192,224},{224,1... | collective-permute-start | bytes 1572872 | tf_op jit(solution)/shard_map/ppermute | solution.py:19
  165.1 0.8 copy-start.4
  168.2 81.2 %copy-start.2 = (bf16[2,8,128,128]{3,2,1,0:T(8,128)(2,1)S(1)}, bf16[2,8,128,128]{3,2,1,0:T(8,128)(2,1)}, u32[]{:S(2)}) copy-start(bf16[2,8,128,128]{3,2,1,0:T(8,128)(2,1)} %copy-done.1) | copy-start | bytes 1572868
  190.9 58.5 %all-to-all-start.2 = ((bf16[32,1,128,128]{3,2,1,0:T(8,128)(2,1)}), bf16[32,1,128,128]{3,2,1,0:T(8,128)(2,1)S(1)}, u32[]{:S(2)}, u32[]{:S(2)}) async-start(bf16[32,1,128,128]{3,2,1,0:T(8,128)(2,1)} %pick_d.1), calls=%async_computation.2 | async-start | bytes 2097152 | tf_op jit(solution)/shard_map/all_to_all | solution.py:33
